TPU v7x, 256 devices: a whole 4x4x8 slice. The times are simulated.
256 devices in a mesh: role: 2 (over core), dp: 16 (over z, x_hi), mp: 8 (over x_lo, y).
Axes of the slice: x: 4 (x_hi: 2, x_lo: 2; x = x_hi * 2 + x_lo), y: 4, z: 8, core: 2. Of those that a mesh axis runs over, the one named last changes fastest.
Arguments:
- tokens: bfloat16 [384, 8192], P('mp', 'dp'), may hold values from -50 to 50
- gate_up: bfloat16 [2, 8192, 2, 14336], P('role', 'dp', None, 'mp'), may hold values from -0.0625 to 0.0625
- down: bfloat16 [2, 14336, 8192], P('role', 'mp', 'dp'), may hold values from -0.046875 to 0.046875
- linear: bfloat16 [8192, 8192], P('dp', 'mp'), may hold values from -0.0625 to 0.0625
Outputs:
- gate_up_grad: bfloat16 [2, 8192, 14336], P('role', 'dp', 'mp')
- down_grad: bfloat16 [14336, 8192], P('mp', 'dp')
- linear_grad: bfloat16 [8192, 8192], P('dp', 'mp')
- losses: float32 [2], replicated
All inputs are finite; a program needn't handle non-finite values.
Results may differ from a plain program's by a relative error of at most 0.015.
Values may be sent and summed in bfloat16 or wider, within the bound.
A program may use at most 128 MiB of HBM per device.

v0:
```python
import jax
import jax.numpy as jnp
from jax import lax
from jax.sharding import PartitionSpec as P

D = 8192


def from_partner(shard, axis, apart):
    return lax.ppermute(shard, axis, [(i, i ^ 1 << apart) for i in range(lax.axis_size(axis))])


def passed_along(block, axis, distance):
    devices = range(lax.axis_size(axis))
    route = [(i - distance, i) for i in devices if i - distance in devices]
    return lax.ppermute(block, axis, route)


def contract_rows(left, right):
    return lax.dot_general(
        left, right, (((0,), (0,)), ((), ())), preferred_element_type=jnp.float32
    )


def body(tokens, gate_up, down, linear):
    is_student = lax.axis_index("role") == 1
    tok_rows = lax.all_gather(tokens, "mp", axis=0, tiled=True)
    unit_count = gate_up.shape[3]
    weight_in = gate_up[0].reshape(gate_up.shape[1], 2 * unit_count)
    weight_out = down[0]
    row_block = tok_rows
    pre_act = lax.psum_scatter(
        jnp.dot(row_block, weight_in, preferred_element_type=jnp.float32),
        "dp",
        scatter_dimension=0,
        tiled=True,
    )
    pre_act = pre_act.reshape(pre_act.shape[0], 2, unit_count)
    gate_pre = pre_act[:, 0]
    up_pre = pre_act[:, 1]
    gate_sig = jax.nn.sigmoid(gate_pre)
    hidden = (gate_pre * gate_sig * up_pre).astype(jnp.bfloat16)
    hidden_all = lax.all_gather(hidden, "dp", axis=0, tiled=True)
    row_block = hidden_all
    own_rows = lax.psum_scatter(
        jnp.dot(row_block, weight_out, preferred_element_type=jnp.float32),
        "mp",
        scatter_dimension=0,
        tiled=True,
    ).astype(jnp.bfloat16)
    row_block = tok_rows
    linear_rows = lax.psum_scatter(
        jnp.dot(row_block, linear, preferred_element_type=jnp.float32).astype(jnp.bfloat16),
        "dp",
        scatter_dimension=0,
        tiled=True,
    ).astype(jnp.float32)
    partner = from_partner(own_rows, "role", 0)
    teacher_rows = jnp.where(is_student, partner, own_rows)
    student_rows = jnp.where(is_student, own_rows, partner)
    target_all = lax.all_gather(teacher_rows, "mp", axis=0, tiled=True)
    spread = lax.all_to_all(target_all, "dp", split_axis=0, concat_axis=1, tiled=True)
    col_count = linear.shape[1]
    target_lin = lax.dynamic_slice_in_dim(spread, lax.axis_index("mp") * col_count, col_count, 1)
    teacher_float = teacher_rows.astype(jnp.float32)
    error_ffn = student_rows.astype(jnp.float32) - teacher_float
    error_lin = linear_rows - target_lin.astype(jnp.float32)
    statistics = lax.psum(
        (
            jnp.sum(teacher_float * teacher_float),
            jnp.sum(error_ffn * error_ffn),
            jnp.sum(error_lin * error_lin),
        ),
        ("dp", "mp"),
    )
    target_norm = statistics[0]
    losses = jnp.stack([statistics[1] / target_norm, statistics[2] / target_norm])
    factor = 16.0 * D / target_norm
    cot_ffn = (factor * error_ffn).astype(jnp.bfloat16)
    cot_lin = (factor * error_lin).astype(jnp.bfloat16)
    cot_ffn_all = lax.all_gather(cot_ffn, "mp", axis=0, tiled=True)
    cot_lin_all = lax.all_gather(cot_lin, "dp", axis=0, tiled=True)
    row_block = cot_ffn_all
    hidden_cot = lax.psum_scatter(
        lax.dot_general(
            row_block, weight_out, (((1,), (1,)), ((), ())), preferred_element_type=jnp.float32
        ),
        "dp",
        scatter_dimension=0,
        tiled=True,
    )
    gate_cot = hidden_cot * up_pre * gate_sig * (1.0 + gate_pre * (1.0 - gate_sig))
    up_cot = hidden_cot * gate_pre * gate_sig
    unit_cot = jnp.stack([gate_cot, up_cot], axis=1).astype(jnp.bfloat16)
    unit_cot_all = lax.all_gather(unit_cot, "dp", axis=0, tiled=True)
    unit_grad = jnp.einsum(
        "td,tgf->gdf", tok_rows, unit_cot_all, preferred_element_type=jnp.float32
    ).astype(jnp.bfloat16)
    down_own = contract_rows(hidden_all, cot_ffn_all).astype(jnp.bfloat16)
    linear_own = contract_rows(tok_rows, cot_lin_all).astype(jnp.bfloat16)
    sent = passed_along((unit_grad[0], down_own, linear_own), "role", -1)
    gate_up_grad = jnp.where(is_student, unit_grad[1:2], sent[0][None])
    down_out = jnp.where(is_student, down_own, sent[1])
    linear_out = jnp.where(is_student, linear_own, sent[2])
    return (gate_up_grad, down_out, linear_out, losses)


def solution(mesh):
    return jax.shard_map(
        body,
        mesh=mesh,
        in_specs=(P("mp", "dp"), P("role", "dp", None, "mp"), P("role", "mp", "dp"), P("dp", "mp")),
        out_specs=(P("role", "dp", "mp"), P("mp", "dp"), P("dp", "mp"), P()),
        check_vma=False,
    )
```

profile of v0, /device:TPU:1, one launch (start us, length us, event | category | flops | bytes accessed | tf_op | source)
XLA Modules:
  0.0 1308.8 jit_solution(5223638327362078404)
XLA Ops:
  7.2 24.6 %all_gather.18 = bf16[384,512]{1,0:T(8,128)(2,1)S(1)} all-gather(bf16[48,512]{1,0:T(8,128)(2,1)} %param.4), channel_id=1, replica_groups=mesh['role'=2,'dp'=16,'mp'=8] {'mp'}, dimensions={0}, use_global_device_ids=true | all-gather | bytes 442368 | tf_op jit(solution)/shard_map/all_gather | solution.py:27
  34.5 4.0 fusion.11
  38.6 221.4 %reduce-scatter.5.cloned.1.call-done = f32[24,3584]{1,0:T(8,128)} async-done(((f32[384,3584]{1,0:T(8,128)}), f32[24,3584]{1,0:T(8,128)}) %reduce-scatter.5.cloned.1.call-update) | async-done | bytes 344080 | tf_op jit(solution)/shard_map/reduce_scatter | solution.py:32
  262.3 80.5 %all-gather.3.cloned.1.call-done = bf16[384,1792]{1,0:T(8,128)(2,1)} async-done(((bf16[24,1792]{1,0:T(8,128)(2,1)}), bf16[384,1792]{1,0:T(8,128)(2,1)}) %all-gather.3.cloned.1.call-update) | async-done | bytes 1376272 | tf_op jit(solution)/shard_map/all_gather | solution.py:43
  342.8 3.1 fusion.3
  348.6 33.5 %reduce-scatter.7.cloned.1.call-done = f32[48,512]{1,0:T(8,128)} async-done(((f32[384,512]{1,0:T(8,128)}), f32[48,512]{1,0:T(8,128)}) %reduce-scatter.7.cloned.1.call-update) | async-done | bytes 98320 | tf_op jit(solution)/shard_map/reduce_scatter | solution.py:45
  383.1 5.8 collective-permute-start
  391.3 24.7 %all_gather.22 = bf16[384,512]{1,0:T(8,128)(2,1)} all-gather(bf16[48,512]{1,0:T(8,128)(2,1)S(1)} %get-tuple-element.13), channel_id=1, replica_groups=mesh['role'=2,'dp'=16,'mp'=8] {'mp'}, dimensions={0}, use_global_device_ids=true | all-gather | bytes 442368 | tf_op jit(solution)/shard_map/all_gather | solution.py:61
  416.0 9.0 all-to-all-start
  425.0 12.5 all-to-all-done
  437.6 151.7 %reduce-scatter.11.cloned.1.call-done = bf16[24,1024]{1,0:T(8,128)(2,1)} async-done(((bf16[384,1024]{1,0:T(8,128)(2,1)}), bf16[24,1024]{1,0:T(8,128)(2,1)}) %reduce-scatter.11.cloned.1.call-update) | async-done | bytes 49168 | tf_op jit(solution)/shard_map/reduce_scatter | solution.py:52
  590.8 292.0 %all-reduce = (f32[]{:T(128)}, f32[]{:T(128)}, f32[]{:T(128)}) all-reduce(f32[]{:T(128)} %get-tuple-element.9, f32[]{:T(128)} %multiply_reduce_fusion, f32[]{:T(128)} %get-tuple-element.8), channel_id=1, replica_groups=mesh['role'=2,'dp'=16,'mp'=8] {'dp','mp'}, use_global_device_ids=true, to_apply=%region_3.4 | all-reduce | flops 3 | bytes 24 | tf_op jit(solution)/shard_map/psum | solution.py:68
  883.5 22.5 %all_gather.20 = bf16[384,512]{1,0:T(8,128)(2,1)S(1)} all-gather(bf16[48,512]{1,0:T(8,128)(2,1)S(1)} %multiply_convert_fusion.4), channel_id=1, replica_groups=mesh['role'=2,'dp'=16,'mp'=8] {'mp'}, dimensions={0}, use_global_device_ids=true | all-gather | bytes 442368 | tf_op jit(solution)/shard_map/all_gather | solution.py:81
  908.5 271.8 %reduce-scatter.9.cloned.1.call-done = f32[24,1792]{1,0:T(8,128)} async-done(((f32[384,1792]{1,0:T(8,128)}), f32[24,1792]{1,0:T(8,128)}) %reduce-scatter.9.cloned.1.call-update) | async-done | bytes 172048 | tf_op jit(solution)/shard_map/reduce_scatter | solution.py:84
  1182.1 3.7 convolution_convert_fusion.1
  1185.8 7.9 collective-permute-start.2
  1193.7 38.1 %all_gather.23 = bf16[384,1024]{1,0:T(8,128)(2,1)S(1)} all-gather(bf16[24,1024]{1,0:T(8,128)(2,1)S(1)} %multiply_convert_fusion.3), channel_id=1, replica_groups=mesh['role'=2,'dp'=16,'mp'=8] {'dp'}, dimensions={0}, use_global_device_ids=true | all-gather | bytes 835584 | tf_op jit(solution)/shard_map/all_gather | solution.py:82
  1232.5 6.2 collective-permute-start.3
  1238.7 34.1 %all-gather.5.cloned.1.call-done = bf16[384,2,1792]{2,0,1:T(8,128)(2,1)} async-done(((bf16[24,2,1792]{2,0,1:T(8,128)(2,1)}), bf16[384,2,1792]{2,0,1:T(8,128)(2,1)}) %all-gather.5.cloned.1.call-update) | async-done | bytes 2752528 | tf_op jit(solution)/shard_map/all_gather | solution.py:95
  1272.9 3.9 fusion
  1279.1 7.2 collective-permute-start.1
  1292.2 3.1 broadcast_select_fusion
  1295.2 3.0 slice_select_fusion
  1298.2 3.8 copy.11
  (47 shorter events, 23.2 us)
Async XLA Ops:
  7.2 335.6 %copy-start = (bf16[1,1792,512]{2,1,0:T(8,128)(2,1)S(1)}, bf16[1,1792,512]{2,1,0:T(8,128)(2,1)}, u32[]{:S(2)}) copy-start(bf16[1,1792,512]{2,1,0:T(8,128)(2,1)} %param.6) | copy-start | bytes 5505028
  7.2 252.9 %reduce-scatter.5.cloned.1.call-start = ((), (), s32[]{:S(2)}) async-start(), calls=%async_computation.5 | async-start | bytes 5849088 | tf_op jit(solution)/shard_map/reduce_scatter | solution.py:32
  38.5 304.2 %all-gather.3.cloned.1.call-start = ((), (), s32[]{:S(2)}) async-start(), calls=%async_computation.6 | async-start | bytes 1462272 | tf_op jit(solution)/shard_map/all_gather | solution.py:43
  262.2 119.9 %reduce-scatter.7.cloned.1.call-start = ((), (), s32[]{:S(2)}) async-start(), calls=%async_computation.7 | async-start | bytes 884736 | tf_op jit(solution)/shard_map/reduce_scatter | solution.py:45
  345.9 243.5 %reduce-scatter.11.cloned.1.call-start = ((), (), s32[]{:S(2)}) async-start(), calls=%async_computation.10 | async-start | bytes 835584 | tf_op jit(solution)/shard_map/reduce_scatter | solution.py:52
  382.1 501.3 %copy-start.4 = (f32[48,512]{1,0:T(8,128)S(1)}, f32[48,512]{1,0:T(8,128)}, u32[]{:S(2)}) copy-start(f32[48,512]{1,0:T(8,128)} %reduce-scatter.7.cloned.1.call-done) | copy-start | bytes 294916
  383.1 6.7 collective-permute-start
  416.0 21.6 %all-to-all-start = ((bf16[16,24,512]{2,1,0:T(8,128)(2,1)}), bf16[16,24,512]{2,1,0:T(8,128)(2,1)S(1)}, u32[]{:S(2)}, u32[]{:S(2)}) async-start(bf16[16,24,512]{2,1,0:T(8,128)(2,1)} %bitcast.9), calls=%async_computation.4 | async-start | bytes 786432 | tf_op jit(solution)/shard_map/all_to_all | solution.py:62
  425.0 755.3 %reduce-scatter.9.cloned.1.call-start = ((), (), s32[]{:S(2)}) async-start(), calls=%async_computation.8 | async-start | bytes 2924544 | tf_op jit(solution)/shard_map/reduce_scatter | solution.py:84
  908.4 364.4 %all-gather.5.cloned.1.call-start = ((), (), s32[]{:S(2)}) async-start(), calls=%async_computation.9 | async-start | bytes 2924544 | tf_op jit(solution)/shard_map/all_gather | solution.py:95
  1182.1 11.6 copy-start.5
  1185.8 106.4 %collective-permute-start.2 = (bf16[1792,512]{1,0:T(8,128)(2,1)}, bf16[1792,512]{1,0:T(8,128)(2,1)}, u32[]{:S(2)}, u32[]{:S(2)}) collective-permute-start(bf16[1792,512]{1,0:T(8,128)(2,1)} %convolution_convert_fusion.1), channel_id=1, source_target_pairs={{128,0},{129,1},{130,2},{131,3},{132,4},{133,5},{134,6},{135,7},{1... | collective-permute-start | bytes 5505032 | tf_op jit(solution)/shard_map/ppermute | solution.py:16
  1232.5 45.7 %copy-start.3 = (bf16[512,1024]{0,1:T(8,128)(2,1)}, bf16[512,1024]{0,1:T(8,128)(2,1)S(1)}, u32[]{:S(2)}) copy-start(bf16[512,1024]{0,1:T(8,128)(2,1)S(1)} %fusion.5) | copy-start | bytes 3145732
  1232.5 57.0 %collective-permute-start.3 = (bf16[512,1024]{0,1:T(8,128)(2,1)S(1)}, bf16[512,1024]{0,1:T(8,128)(2,1)}, u32[]{:S(2)}, u32[]{:S(2)}) collective-permute-start(bf16[512,1024]{0,1:T(8,128)(2,1)S(1)} %fusion.5), channel_id=1, source_target_pairs={{128,0},{129,1},{130,2},{131,3},{132,4},{133,5},{134,6},{135,7},{1... | collective-permute-start | bytes 3145736 | tf_op jit(solution)/shard_map/ppermute | solution.py:16
  1276.8 2.4 copy-start.1
  1279.1 16.1 %collective-permute-start.1 = (bf16[512,1792]{0,1:T(8,128)(2,1)}, bf16[512,1792]{0,1:T(8,128)(2,1)}, u32[]{:S(2)}, u32[]{:S(2)}) collective-permute-start(bf16[512,1792]{0,1:T(8,128)(2,1)} %slice_bitcast_fusion), channel_id=1, source_target_pairs={{128,0},{129,1},{130,2},{131,3},{132,4},{133,5},{134,6},{135,7},{1... | collective-permute-start | bytes 5505032 | tf_op jit(solution)/shard_map/ppermute | solution.py:16
  1292.2 3.1 copy-start.2
Sparse Core Ops, SparseCore 0:
  38.7 221.3 reduce-scatter.4
  263.6 79.1 all-gather.2
  346.0 36.0 reduce-scatter.6
  386.4 202.9 reduce-scatter.10
  908.6 271.7 reduce-scatter.8
  1183.8 89.0 all-gather.4
where the time goes:
time: 1310 us
  waiting for transfers between devices  807 us (62%)
  blocking collectives  402 us (31%)
  starting transfers between devices  36.4 us (3%)
  matrix products  20.6 us (2%)
  between operations  17.4 us (1%)
  other arithmetic  14.3 us (1%)
    psum x1, blocking collectives, body(): lax.psum((jnp.sum(teacher_float * teacher_float), jnp.sum(error_ffn * err...  292 us
    reduce_scatter x1, waiting for transfers between devices, body(): lax.psum_scatter(lax.dot_general(row_block, weight_out, (((1,), (1,)), ((...  272 us
    reduce_scatter x1, waiting for transfers between devices, body(): lax.psum_scatter(jnp.dot(row_block, weight_in, preferred_element_type=jnp...  221 us
    reduce_scatter x1, waiting for transfers between devices, body(): lax.psum_scatter(jnp.dot(row_block, linear, preferred_element_type=jnp.fl...  152 us
    all_gather x1, waiting for transfers between devices, body(): hidden_all = lax.all_gather(hidden, 'dp', axis=0, tiled=True)  80.5 us
    all_gather x1, blocking collectives, body(): cot_lin_all = lax.all_gather(cot_lin, 'dp', axis=0, tiled=True)  38.1 us
    all_gather x1, waiting for transfers between devices, body(): unit_cot_all = lax.all_gather(unit_cot, 'dp', axis=0, tiled=True)  34.1 us
    reduce_scatter x1, waiting for transfers between devices, body(): lax.psum_scatter(jnp.dot(row_block, weight_out, preferred_element_type=jn...  33.5 us
  transfers between devices with their start and end apart: 11, of which 8 were waited for; matrix products, arithmetic and copies ran while one was open for 2% of the time, Pallas kernels for 0%

commit v1 on v0

v1 whole, which is shorter than its diff:
```python
import jax
import jax.numpy as jnp
from jax import lax
from jax.experimental import pallas as pl
from jax.experimental.pallas import tpu as pltpu
from jax.sharding import PartitionSpec as P

MESH = pl.DeviceIdType.MESH
BF16, F32 = jnp.bfloat16, jnp.float32
MODEL = 8192
Z = 8
ROWS = 48
WIDTH = 512
UNITS = 1792
HALF = UNITS // 2
LIN = 1024
QUARTER = LIN // 4


def remote(src, dst, send, recv, device):
    return pltpu.make_async_remote_copy(
        src_ref=src, dst_ref=dst, send_sem=send, recv_sem=recv, device_id=device, device_id_type=MESH
    )


class RingSum:
    def __init__(self, place, part, out, into, send, recv, tags, long_way):
        self.place, self.part, self.out, self.into = place, part, out, into
        self.send, self.recv, self.tags, self.long_way = send, recv, tags, long_way

    def copy(self, way, step, tag):
        at = (way, step - 1) + tag
        return remote(
            self.out.at[at], self.into.at[at], self.send.at[at], self.recv.at[at], self.place.z_next[way]
        )

    def push(self, way, step, tag, first):
        sign = 1 - 2 * way
        block = lax.rem(self.place.z + sign * (5 - step) + Z, Z)
        total = self.part[tag + (block,)]
        if not first:
            self.copy(way, step - 1, tag).wait_recv()
            total = total + self.into[(way, step - 2) + tag].astype(F32)
        self.out[(way, step - 1) + tag] = total.astype(BF16)
        self.copy(way, step, tag).start()

    def begin(self, tag):
        far = self.long_way(tag)
        self.push(far, 1, tag, True)
        self.push(1 - far, 2, tag, True)

    def step(self, step):
        for tag in self.tags:
            for way in (0, 1):
                if step > 2 or way == self.long_way(tag):
                    self.push(way, step, tag, False)

    def result(self, tag):
        total = self.part[tag + (self.place.z,)]
        for way in (0, 1):
            self.copy(way, 4, tag).wait_recv()
            total = total + self.into[(way, 3) + tag].astype(F32)
        return total

    def drain(self):
        for tag in self.tags:
            for way in (0, 1):
                for step in range(1 if way == self.long_way(tag) else 2, 5):
                    self.copy(way, step, tag).wait_send()


class RingGather:
    def __init__(self, place, buf, send, recv, x_send, x_recv):
        self.place, self.buf, self.send, self.recv = place, buf, send, recv
        self.x_send, self.x_recv = x_send, x_recv

    def copy(self, way, step, mine, arriving=False):
        place = self.place
        sign = 1 - 2 * way
        block = lax.rem(place.z - sign * (step if arriving else step - 1) + Z, Z)
        x = place.x if mine else 1 - place.x
        part = self.buf.at[block, x]
        at = (way, step - 1, mine)
        return remote(part, part, self.send.at[at], self.recv.at[at], place.z_next[way])

    def x_copy(self, arriving=False):
        place = self.place
        part = self.buf.at[place.z, 1 - place.x if arriving else place.x]
        return remote(part, part, self.x_send, self.x_recv, place.x_other)

    def begin(self):
        self.copy(0, 1, 1).start()
        self.copy(1, 1, 1).start()
        self.x_copy().start()

    def begin_other(self):
        self.x_copy(True).wait_recv()
        self.copy(0, 1, 0).start()
        self.copy(1, 1, 0).start()

    def step(self, step):
        for mine in (1, 0):
            for way in (0, 1):
                self.copy(way, step, mine, True).wait_recv()
                if step < 3 or way == 1 - mine:
                    self.copy(way, step + 1, mine).start()

    def last(self):
        for mine in (1, 0):
            self.copy(1 - mine, 4, mine, True).wait_recv()

    def drain(self):
        self.x_copy().wait_send()
        for mine in (1, 0):
            for way in (0, 1):
                for step in range(1, 5 if way == 1 - mine else 4):
                    self.copy(way, step, mine).wait_send()


class Direct:
    def __init__(self, me, device_of, out, into, send, recv):
        self.me, self.device_of, self.out, self.into, self.send, self.recv = me, device_of, out, into, send, recv

    def copy(self, apart):
        peer = lax.rem(self.me + apart, 8)
        return remote(
            self.out(peer), self.into(self.me), self.send.at[apart - 1], self.recv.at[apart - 1], self.device_of(peer)
        )

    def start(self):
        for apart in (4, 3, 5, 2, 6, 1, 7):
            self.copy(apart).start()

    def wait(self):
        for apart in (1, 7, 2, 6, 3, 5, 4):
            source = lax.rem(self.me - apart + 8, 8)
            part = self.into(source)
            remote(
                part, part, self.send.at[apart - 1], self.recv.at[apart - 1], self.device_of(source)
            ).wait_recv()

    def drain(self):
        for apart in range(1, 8):
            self.copy(apart).wait_send()


class Place:
    def __init__(self):
        self.role, self.mp = lax.axis_index("role"), lax.axis_index("mp")
        dp = lax.axis_index("dp")
        self.z, self.x = dp // 2, lax.rem(dp, 2)
        role, mp, z, x = self.role, self.mp, self.z, self.x
        self.z_next = ((role, lax.rem(z + 1, Z) * 2 + x, mp), (role, lax.rem(z + Z - 1, Z) * 2 + x, mp))
        self.x_other = (role, z * 2 + 1 - x, mp)
        self.partner = (1 - role, dp, mp)
        self.across = (role, mp * 2 + x, z)
        self.of_z = lambda peer: (role, peer * 2 + x, mp)
        self.of_mp = lambda peer: (role, dp, peer)


def exchange_kernel(
    tok_in, w_in, down_in, lin_in,
    tok_out, cot_out, hid_out, err_out, lin_out, stat_out,
    tok, w, down, lin,
    part, b_out, b_into, bx_out, bx_into, pre, hid,
    d_out, d_into, rows, rows_other, err, target_out, target,
    lin_part, e_out, e_into, ex_out, ex_into, lin_err,
    k_out, k_into, kx_out, kx_into, gate_out, cot,
    m_stat, z_stat, x_stat, x_stat_other, r_stat, r_stat_other,
    load_sem, store_sem,
    tok_s, tok_r, b_s, b_r, bx_s, bx_r, c_s, c_r, cx_s, cx_r,
    d_s, d_r, one_s, one_r, i_s, i_r, e_s, e_r, k_s, k_r,
    j_s, j_r, l_s, l_r, m_s, m_r, z_s, z_r, share_s, share_r,
):
    place = Place()
    role, mp, z, x = place.role, place.mp, place.z, place.x
    student, teacher = role == 1, role == 0
    x_of = (1 - x, x)

    loads = [
        pltpu.make_async_copy(tok_in, tok.at[mp], load_sem.at[0]),
        pltpu.make_async_copy(w_in, w, load_sem.at[1]),
        pltpu.make_async_copy(down_in, down, load_sem.at[2]),
    ] + [
        pltpu.make_async_copy(
            lin_in.at[:, pl.ds(pl.multiple_of(b * 2 * QUARTER + role * QUARTER, QUARTER), QUARTER)],
            lin.at[b],
            load_sem.at[3 + b],
        )
        for b in (0, 1)
    ]
    for load in loads:
        load.start()

    barrier = pltpu.get_barrier_semaphore()

    def greet(device):
        pl.semaphore_signal(barrier, inc=1, device_id=device, device_id_type=MESH)

    for apart in range(1, 8):
        greet(place.of_mp(lax.rem(mp + apart, 8)))
        greet(place.of_z(lax.rem(z + apart, 8)))
    greet(place.x_other)
    greet(place.partner)

    @pl.when(z != mp)
    def _():
        greet(place.across)
        pl.semaphore_wait(barrier, 17)

    @pl.when(z == mp)
    def _():
        pl.semaphore_wait(barrier, 16)

    loads[0].wait()
    tokens = Direct(mp, place.of_mp, lambda peer: tok.at[mp], lambda source: tok.at[source], tok_s, tok_r)
    tokens.start()
    loads[1].wait()
    tokens.wait()
    stores = [pltpu.make_async_copy(tok, tok_out, store_sem.at[0])]
    stores[0].start()
    all_tok = tok[...].reshape(Z * ROWS, WIDTH)

    tags = [(q, g) for q in (0, 1) for g in (0, 1)]
    b_sum = RingSum(place, part, b_out, b_into, b_s, b_r, tags, lambda tag: tag[1])
    for q, g in tags:
        column = pl.multiple_of(g * UNITS + x_of[q] * HALF, 128)
        part[q, g] = jnp.dot(
            tok[...].reshape(Z * ROWS, WIDTH), w[:, pl.ds(column, HALF)], preferred_element_type=F32
        ).reshape(Z, ROWS, HALF)
        b_sum.begin((q, g))
    b_sum.step(2)
    for load in loads[2:]:
        load.wait()
    for q in (0, 1):
        lin_part[q] = jnp.dot(
            tok[...].reshape(Z * ROWS, WIDTH), lin[x_of[q]], preferred_element_type=F32
        ).reshape(Z, ROWS, QUARTER)
    b_sum.step(3)
    b_sum.step(4)

    def bx_copy(g):
        return remote(bx_out.at[g], bx_into.at[g], bx_s.at[g], bx_r.at[g], place.x_other)

    for g in (0, 1):
        bx_out[g] = b_sum.result((0, g)).astype(BF16)
        bx_copy(g).start()
    for g in (0, 1):
        pre[g] = b_sum.result((1, g))
    for g in (0, 1):
        bx_copy(g).wait_recv()
        pre[g] = pre[g] + bx_into[g].astype(F32)
    gate = pre[0]
    hid[z, x] = (gate * jax.nn.sigmoid(gate) * pre[1]).astype(BF16)

    c_all = RingGather(place, hid, c_s, c_r, cx_s.at[0], cx_r.at[0])
    c_all.begin()
    c_all.begin_other()
    for step in (1, 2, 3):
        c_all.step(step)
    e_sum = RingSum(place, lin_part, e_out, e_into, e_s, e_r, [(0,), (1,)], lambda tag: tag[0])
    for tag in e_sum.tags:
        e_sum.begin(tag)
    c_all.last()

    outputs = jnp.zeros((Z * ROWS, WIDTH), F32)
    for b in (0, 1):
        outputs += jnp.dot(
            hid[:, b].reshape(Z * ROWS, HALF), down[b * HALF : (b + 1) * HALF], preferred_element_type=F32
        )
    d_out[...] = outputs.reshape(Z, ROWS, WIDTH).astype(BF16)
    d_sum = Direct(mp, place.of_mp, lambda peer: d_out.at[peer], lambda source: d_into.at[source], d_s, d_r)
    d_sum.start()
    d_into[mp] = d_out[mp]
    e_sum.step(2)

    def hid_share(b):
        return remote(
            hid.at[:, b], hid_out.at[:, :, b * HALF : (b + 1) * HALF], share_s.at[b], share_r.at[b], place.partner
        )

    def hid_store(b):
        return pltpu.make_async_copy(hid.at[:, b], hid_out.at[:, :, b * HALF : (b + 1) * HALF], store_sem.at[1 + b])

    @pl.when(student)
    def _():
        for b in (0, 1):
            hid_share(b).start()
            hid_store(b).start()

    d_sum.wait()
    own = d_into[0].astype(F32)
    for source in range(1, 8):
        own = own + d_into[source].astype(F32)
    rows[...] = own.astype(BF16)

    def rows_copy():
        return remote(rows, rows_other, one_s.at[0], one_r.at[0], place.partner)

    rows_copy().start()
    e_sum.step(3)
    rows_copy().wait_recv()
    mine, other = rows[...].astype(F32), rows_other[...].astype(F32)
    teacher_rows = jnp.where(student, other, mine)
    error = jnp.where(student, mine - other, other - mine)
    err[mp] = error.astype(BF16)
    err_all = Direct(mp, place.of_mp, lambda peer: err.at[mp], lambda source: err.at[source], i_s, i_r)

    @pl.when(student)
    def _():
        err_all.start()

    for b in (0, 1):
        target_out[b] = teacher_rows[:, b * QUARTER : (b + 1) * QUARTER].astype(BF16)

    def target_copy():
        return remote(target_out.at[role], target, one_s.at[1], one_r.at[1], place.across)

    @pl.when(z != mp)
    def _():
        target_copy().start()

    @pl.when(z == mp)
    def _():
        target[...] = target_out[role]

    target_square = jnp.sum(teacher_rows * teacher_rows)
    error_square = jnp.sum(error * error)
    e_sum.step(4)

    def err_share():
        return remote(err, err_out, share_s.at[2], share_r.at[2], place.partner)

    def err_store():
        return pltpu.make_async_copy(err, err_out, store_sem.at[3])

    k_sum = RingSum(place, part.at[:, 0], k_out, k_into, k_s, k_r, [(0,), (1,)], lambda tag: tag[0])

    @pl.when(student)
    def _():
        err_all.wait()
        err_share().start()
        err_store().start()
        for q in (0, 1):
            start = pl.multiple_of(x_of[q] * HALF, 128)
            part[q, 0] = lax.dot_general(
                err[...].reshape(Z * ROWS, WIDTH),
                down[pl.ds(start, HALF)],
                (((1,), (1,)), ((), ())),
                preferred_element_type=F32,
            ).reshape(Z, ROWS, HALF)
            k_sum.begin((q,))

    def ex_copy():
        return remote(ex_out, ex_into, one_s.at[2], one_r.at[2], place.x_other)

    ex_out[...] = e_sum.result((0,)).astype(BF16)
    ex_copy().start()
    linear_rows = e_sum.result((1,))

    @pl.when(student)
    def _():
        k_sum.step(2)

    ex_copy().wait_recv()

    @pl.when(z != mp)
    def _():
        target_copy().wait_recv()

    linear_error = linear_rows + ex_into[...].astype(F32) - target[...].astype(F32)
    lin_err[z, x] = linear_error.astype(BF16)
    linear_square = jnp.sum(linear_error * linear_error)
    row = lax.broadcasted_iota(jnp.int32, (8, 128), 0)
    m_stat[mp] = jnp.where(row == 0, target_square, jnp.where(row == 1, error_square, linear_square))
    m_all = Direct(mp, place.of_mp, lambda peer: m_stat.at[mp], lambda source: m_stat.at[source], m_s, m_r)
    m_all.start()

    @pl.when(student)
    def _():
        k_sum.step(3)

    def in_order(slots):
        total = slots[0]
        for source in range(1, 8):
            total = total + slots[source]
        return total

    def x_stat_copy():
        return remote(x_stat, x_stat_other, one_s.at[3], one_r.at[3], place.x_other)

    m_all.wait()
    x_stat[...] = in_order(m_stat)
    x_stat_copy().start()

    @pl.when(student)
    def _():
        k_sum.step(4)

    x_stat_copy().wait_recv()
    z_stat[z] = x_stat[...] + x_stat_other[...]
    z_all = Direct(z, place.of_z, lambda peer: z_stat.at[z], lambda source: z_stat.at[source], z_s, z_r)
    z_all.start()
    j_all = RingGather(place, lin_err, j_s, j_r, cx_s.at[1], cx_r.at[1])

    def kx_copy():
        return remote(kx_out, kx_into, one_s.at[4], one_r.at[4], place.x_other)

    @pl.when(student)
    def _():
        kx_out[...] = k_sum.result((0,)).astype(BF16)
        kx_copy().start()

    def r_stat_copy():
        return remote(r_stat, r_stat_other, one_s.at[5], one_r.at[5], place.partner)

    z_all.wait()
    r_stat[...] = in_order(z_stat)
    r_stat_copy().start()
    r_stat_copy().wait_recv()
    row_total = r_stat[...] + r_stat_other[...]
    stat = jnp.where(row == 2, row_total, jnp.where(student, r_stat_other[...], r_stat[...]))
    x_stat_other[...] = stat
    stat_store = pltpu.make_async_copy(x_stat_other, stat_out, store_sem.at[4])
    stat_store.start()
    factor = (16.0 * MODEL) / stat[0:1, 0:1]

    def gate_copy():
        return remote(gate_out, cot.at[z, x], one_s.at[6], one_r.at[6], place.partner)

    @pl.when(student)
    def _():
        total = k_sum.result((1,))
        kx_copy().wait_recv()
        hidden_cot = (total + kx_into[...].astype(F32)) * factor
        gate_pre, up_pre = pre[0], pre[1]
        sig = jax.nn.sigmoid(gate_pre)
        gate_out[...] = (hidden_cot * up_pre * sig * (1.0 + gate_pre * (1.0 - sig))).astype(BF16)
        gate_copy().start()
        cot[z, x] = (hidden_cot * gate_pre * sig).astype(BF16)

    @pl.when(teacher)
    def _():
        gate_copy().wait_recv()

    l_all = RingGather(place, cot, l_s, l_r, cx_s.at[2], cx_r.at[2])
    l_all.begin()
    j_all.begin()
    l_all.begin_other()
    j_all.begin_other()
    for step in (1, 2, 3):
        l_all.step(step)
        j_all.step(step)
    j_all.last()

    def lin_columns(b):
        start = pl.multiple_of(b * 2 * QUARTER + role * QUARTER, QUARTER)
        return lin_out.at[:, :, pl.ds(start, QUARTER)]

    def lin_share(b):
        return remote(lin_err.at[:, b], lin_columns(b), share_s.at[3 + b], share_r.at[3 + b], place.partner)

    for b in (0, 1):
        lin_share(b).start()
        stores.append(pltpu.make_async_copy(lin_err.at[:, b], lin_columns(b), store_sem.at[5 + b]))
        stores[-1].start()
    l_all.last()
    for b in (0, 1):
        stores.append(
            pltpu.make_async_copy(cot.at[:, b], cot_out.at[:, :, b * HALF : (b + 1) * HALF], store_sem.at[7 + b])
        )
        stores[-1].start()

    tokens.drain()
    b_sum.drain()
    for g in (0, 1):
        bx_copy(g).wait_send()
    c_all.drain()
    d_sum.drain()
    rows_copy().wait_send()
    e_sum.drain()
    ex_copy().wait_send()
    m_all.drain()
    x_stat_copy().wait_send()
    z_all.drain()
    r_stat_copy().wait_send()
    j_all.drain()
    l_all.drain()
    for b in (0, 1):
        lin_share(b).wait_send()

    @pl.when(z != mp)
    def _():
        target_copy().wait_send()

    @pl.when(student)
    def _():
        err_all.drain()
        k_sum.drain()
        kx_copy().wait_send()
        gate_copy().wait_send()
        err_share().wait_send()
        err_store().wait()
        for b in (0, 1):
            hid_share(b).wait_send()
            hid_store(b).wait()

    @pl.when(teacher)
    def _():
        err_share().wait_recv()
        for b in (0, 1):
            hid_share(b).wait_recv()

    for b in (0, 1):
        lin_share(b).wait_recv()
    stat_store.wait()
    for store in stores:
        store.wait()


def exchange(tokens, w, down, linear):
    def vmem(*shape, dtype=BF16):
        return pltpu.VMEM(shape, dtype)

    def sems(*shape):
        return pltpu.SemaphoreType.DMA(shape)

    def array(*shape, dtype=BF16):
        return jax.ShapeDtypeStruct(shape, dtype)

    anywhere = pl.BlockSpec(memory_space=pl.ANY)
    return pl.pallas_call(
        exchange_kernel,
        out_shape=[
            array(Z, ROWS, WIDTH),
            array(Z, ROWS, UNITS),
            array(Z, ROWS, UNITS),
            array(Z, ROWS, WIDTH),
            array(Z, ROWS, LIN),
            array(8, 128, dtype=F32),
        ],
        in_specs=[anywhere] * 4,
        out_specs=[anywhere] * 6,
        scratch_shapes=[
            vmem(Z, ROWS, WIDTH), vmem(WIDTH, 2 * UNITS), vmem(UNITS, WIDTH), vmem(2, WIDTH, QUARTER),
            vmem(2, 2, Z, ROWS, HALF, dtype=F32), vmem(2, 4, 2, 2, ROWS, HALF), vmem(2, 4, 2, 2, ROWS, HALF),
            vmem(2, ROWS, HALF), vmem(2, ROWS, HALF), vmem(2, ROWS, HALF, dtype=F32), vmem(Z, 2, ROWS, HALF),
            vmem(8, ROWS, WIDTH), vmem(8, ROWS, WIDTH), vmem(ROWS, WIDTH), vmem(ROWS, WIDTH),
            vmem(8, ROWS, WIDTH), vmem(2, ROWS, QUARTER), vmem(ROWS, QUARTER),
            vmem(2, Z, ROWS, QUARTER, dtype=F32), vmem(2, 4, 2, ROWS, QUARTER), vmem(2, 4, 2, ROWS, QUARTER),
            vmem(ROWS, QUARTER), vmem(ROWS, QUARTER), vmem(Z, 2, ROWS, QUARTER),
            vmem(2, 4, 2, ROWS, HALF), vmem(2, 4, 2, ROWS, HALF), vmem(ROWS, HALF), vmem(ROWS, HALF),
            vmem(ROWS, HALF), vmem(Z, 2, ROWS, HALF),
            vmem(8, 8, 128, dtype=F32), vmem(8, 8, 128, dtype=F32),
            vmem(8, 128, dtype=F32), vmem(8, 128, dtype=F32), vmem(8, 128, dtype=F32), vmem(8, 128, dtype=F32),
            sems(5), sems(9),
            sems(7), sems(7), sems(2, 4, 2, 2), sems(2, 4, 2, 2), sems(2), sems(2), sems(2, 4, 2), sems(2, 4, 2),
            sems(3), sems(3),
            sems(7), sems(7), sems(7), sems(7), sems(7), sems(7), sems(2, 4, 2), sems(2, 4, 2),
            sems(2, 4, 2), sems(2, 4, 2),
            sems(2, 4, 2), sems(2, 4, 2), sems(2, 4, 2), sems(2, 4, 2), sems(7), sems(7), sems(7), sems(7),
            sems(5), sems(5),
        ],
        compiler_params=pltpu.CompilerParams(
            collective_id=0, has_side_effects=True, vmem_limit_bytes=56 * 1024 * 1024
        ),
        name="exchange",
    )(tokens, w, down, linear)


def contract_rows(left, right):
    return lax.dot_general(left, right, (((0,), (0,)), ((), ())), preferred_element_type=F32)


def body(tokens, gate_up, down, linear):
    w = gate_up.reshape(WIDTH, 2 * UNITS)
    tok, cot, hid, err, lin_err, stat = exchange(tokens, w, down[0], linear)
    tok, cot = tok.reshape(Z * ROWS, WIDTH), cot.reshape(Z * ROWS, UNITS)
    hid, err = hid.reshape(Z * ROWS, UNITS), err.reshape(Z * ROWS, WIDTH)
    lin_err = lin_err.reshape(Z * ROWS, LIN)
    target_norm = stat[0, 0]
    factor = 16.0 * MODEL / target_norm
    gate_up_grad = contract_rows(tok, cot).astype(BF16)[None]
    down_grad = (factor * contract_rows(hid, err)).astype(BF16)
    linear_grad = (factor * contract_rows(tok, lin_err)).astype(BF16)
    losses = jnp.stack([stat[1, 0] / target_norm, stat[2, 0] / target_norm])
    return (gate_up_grad, down_grad, linear_grad, losses)


def solution(mesh):
    return jax.shard_map(
        body,
        mesh=mesh,
        in_specs=(P("mp", "dp"), P("role", "dp", None, "mp"), P("role", "mp", "dp"), P("dp", "mp")),
        out_specs=(P("role", "dp", "mp"), P("mp", "dp"), P("dp", "mp"), P()),
        check_vma=False,
    )
```

time: 1310 us -> 146 us (0.11)
  waiting for transfers between devices: 807 us -> 0 us
  blocking collectives: 402 us -> 0 us
  Pallas kernels: 0 us -> 127 us
  starting transfers between devices: 36.4 us -> 0 us
  other arithmetic: 14.3 us -> 0.59 us
  between operations: 17.4 us -> 4 us
    reduce_scatter x4 -> x0, waiting for transfers between devices: 678 us -> none  [the longest x1 272 us: body(): lax.psum_scatter(lax.dot_general(row_block, weight_out, (((1,), (1,)), ((...]
    psum x1 -> x0, blocking collectives: 292 us -> none  [body(): lax.psum((jnp.sum(teacher_float * teacher_float), jnp.sum(error_ffn * err...]
    pallas_call x0 -> x1, Pallas kernels: none -> 127 us  [exchange(): pl.pallas_call(exchange_kernel, out_shape=[array(Z, ROWS, WIDTH), array(Z...]
    all_gather x2 -> x0, waiting for transfers between devices: 115 us -> none  [the longest x1 80.5 us: body(): hidden_all = lax.all_gather(hidden, 'dp', axis=0, tiled=True)]
    all_gather x4 -> x0, blocking collectives: 110 us -> none  [the longest x1 38.1 us: body(): cot_lin_all = lax.all_gather(cot_lin, 'dp', axis=0, tiled=True)]
    ppermute x4 -> x0, starting transfers between devices: 27.1 us -> none  [the longest x3 21.3 us: passed_along(): return lax.ppermute(block, axis, route)]
    dot_general x5 -> x0, matrix products: 16.1 us -> none  [the longest x1 4.03 us: body(): jnp.dot(row_block, weight_in, preferred_element_type=jnp.float32)]
  transfers between devices with their start and end apart: 11 -> 0, of which waited for: 8 -> 0; matrix products, arithmetic and copies ran while one was open for 2% -> 0% of each run, Pallas kernels for 0% -> 0%
where the time goes in v1:
time: 146 us; the launch traced here: 145 us
  Pallas kernels  127 us (87%)
  matrix products  7.97 us (5%)
  local copies, waits for them, and re-layouts  5.75 us (4%)
  between operations  4 us (3%)
    pallas_call x1, Pallas kernels, exchange(): pl.pallas_call(exchange_kernel, out_shape=[array(Z, ROWS, WIDTH), array(Z...  127 us
    dot_general x3, matrix products, contract_rows(): lax.dot_general(left, right, (((0,), (0,)), ((), ())), preferred_element_...  7.97 us
    unnamed x7, local copies, waits for them, and re-layouts  4.44 us

profile of v1, /device:TPU:1, one launch (start us, length us, event | category | flops | bytes accessed | tf_op | source)
XLA Modules:
  0.0 145.5 jit_solution(15193763640223710015)
XLA Ops:
  0.6 4.4 %copy.8 = bf16[64,8,2,1792]{3,1,2,0:T(8,128)(2,1)} copy(bf16[64,8,2,1792]{3,2,1,0:T(2,128)(2,1)} %bitcast.28) | data formatting | bytes 7340032
  5.1 127.2 %exchange.1 = (bf16[8,48,512]{2,1,0:T(8,128)(2,1)}, bf16[8,48,1792]{2,1,0:T(8,128)(2,1)}, bf16[8,48,1792]{2,1,0:T(8,128)(2,1)}, bf16[8,48,512]{2,1,0:T(8,128)(2,...) custom-call(bf16[48,512]{1,0:T(8,128)(2,1)} %tok_in.1, bf16[512,3584]{1,0:T(8,128)(2,1)} %bitcast.27, ...), custom_call_target="tpu_custom_call" | custom-call | tf_op jit(solution)/shard_map/exchange/pallas_call | solution.py:532
  132.2 1.3 fusion.3
  136.9 0.6 pad_maximum_fusion
  137.5 0.0 copy-start.1
  137.5 0.0 copy-start.2
  137.5 3.9 %fusion = bf16[1792,512]{1,0:T(8,128)(2,1)} fusion(bf16[8,48,1792]{2,1,0:T(8,128)(2,1)} %get-tuple-element.13, bf16[8,48,512]{2,1,0:T(8,128)(2,1)} %get-tuple-element.14, f32[]{:T(128)} %bitcast.3), kind=kOutput, calls=%fused_computation.1 | convolution fusion | flops 706478080 | bytes 3604484 | tf_op jit(solution)/shard_map/dot_general | solution.py:572
  141.4 0.0 copy-done.1
  141.4 0.0 copy-done.2
  141.4 0.0 copy-start
  141.4 1.7 %fusion.2 = bf16[512,1024]{1,0:T(8,128)(2,1)} fusion(bf16[8,48,512]{2,1,0:T(8,128)(2,1)S(1)} %copy-done.2, bf16[8,48,1024]{2,1,0:T(8,128)(2,1)S(1)} %copy-done.1, f32[]{:T(128)} %bitcast.3), kind=kOutput, calls=%fused_computation.5 | convolution fusion | flops 403701760 | bytes 2228228 | tf_op jit(solution)/shard_map/dot_general | solution.py:572
  143.1 0.0 copy-done
  143.1 2.4 %fusion.1 = bf16[1,512,1792]{2,1,0:T(8,128)(2,1)} fusion(bf16[8,48,512]{2,1,0:T(8,128)(2,1)S(1)} %copy-done.2, bf16[8,48,1792]{2,1,0:T(8,128)(2,1)S(1)} %copy-done), kind=kOutput, calls=%fused_computation.3 | convolution fusion | flops 705560576 | bytes 3604480 | tf_op jit(solution)/shard_map/dot_general | solution.py:572
Async XLA Ops:
  137.5 3.9 %copy-start.1 = (bf16[8,48,1024]{2,1,0:T(8,128)(2,1)S(1)}, bf16[8,48,1024]{2,1,0:T(8,128)(2,1)}, u32[]{:S(2)}) copy-start(bf16[8,48,1024]{2,1,0:T(8,128)(2,1)} %get-tuple-element.15) | copy-start | bytes 2359300
  137.5 3.9 %copy-start.2 = (bf16[8,48,512]{2,1,0:T(8,128)(2,1)S(1)}, bf16[8,48,512]{2,1,0:T(8,128)(2,1)}, u32[]{:S(2)}) copy-start(bf16[8,48,512]{2,1,0:T(8,128)(2,1)} %get-tuple-element.10) | copy-start | bytes 1179652
  141.4 1.7 %copy-start = (bf16[8,48,1792]{2,1,0:T(8,128)(2,1)S(1)}, bf16[8,48,1792]{2,1,0:T(8,128)(2,1)}, u32[]{:S(2)}) copy-start(bf16[8,48,1792]{2,1,0:T(8,128)(2,1)} %get-tuple-element.11) | copy-start | bytes 4128772

commit v2 on v1

v2 whole, which is shorter than its diff:
```python
import jax
import jax.numpy as jnp
from jax import lax
from jax.experimental import pallas as pl
from jax.experimental.pallas import tpu as pltpu
from jax.sharding import PartitionSpec as P

MESH = pl.DeviceIdType.MESH
BF16, F32 = jnp.bfloat16, jnp.float32
MODEL = 8192
Z = 8
ROWS = 48
WIDTH = 512
UNITS = 1792
HALF = UNITS // 2
LIN = 1024
QUARTER = LIN // 4


def remote(src, dst, send, recv, device):
    return pltpu.make_async_remote_copy(
        src_ref=src, dst_ref=dst, send_sem=send, recv_sem=recv, device_id=device, device_id_type=MESH
    )


class RingSum:
    def __init__(self, place, part, out, into, send, recv, tags, long_way):
        self.place, self.part, self.out, self.into = place, part, out, into
        self.send, self.recv, self.tags, self.long_way = send, recv, tags, long_way

    def copy(self, way, step, tag):
        at = (way, step - 1) + tag
        return remote(
            self.out.at[at], self.into.at[at], self.send.at[at], self.recv.at[at], self.place.z_next[way]
        )

    def push(self, way, step, tag, first):
        sign = 1 - 2 * way
        block = lax.rem(self.place.z + sign * (5 - step) + Z, Z)
        total = self.part[tag + (block,)]
        if not first:
            self.copy(way, step - 1, tag).wait_recv()
            total = total + self.into[(way, step - 2) + tag].astype(F32)
        self.out[(way, step - 1) + tag] = total.astype(BF16)
        self.copy(way, step, tag).start()

    def begin(self, tag):
        far = self.long_way(tag)
        self.push(far, 1, tag, True)
        self.push(1 - far, 2, tag, True)

    def step(self, step, tags=None):
        for tag in tags or self.tags:
            for way in (0, 1):
                if step > 2 or way == self.long_way(tag):
                    self.push(way, step, tag, False)

    def result(self, tag):
        total = self.part[tag + (self.place.z,)]
        for way in (0, 1):
            self.copy(way, 4, tag).wait_recv()
            total = total + self.into[(way, 3) + tag].astype(F32)
        return total

    def drain(self):
        for tag in self.tags:
            for way in (0, 1):
                for step in range(1 if way == self.long_way(tag) else 2, 5):
                    self.copy(way, step, tag).wait_send()


class RingGather:
    def __init__(self, place, buf, send, recv, x_send, x_recv):
        self.place, self.buf, self.send, self.recv = place, buf, send, recv
        self.x_send, self.x_recv = x_send, x_recv

    def copy(self, way, step, mine, arriving=False):
        place = self.place
        sign = 1 - 2 * way
        block = lax.rem(place.z - sign * (step if arriving else step - 1) + Z, Z)
        x = place.x if mine else 1 - place.x
        part = self.buf.at[block, x]
        at = (way, step - 1, mine)
        return remote(part, part, self.send.at[at], self.recv.at[at], place.z_next[way])

    def x_copy(self, arriving=False):
        place = self.place
        part = self.buf.at[place.z, 1 - place.x if arriving else place.x]
        return remote(part, part, self.x_send, self.x_recv, place.x_other)

    def begin(self):
        self.copy(0, 1, 1).start()
        self.copy(1, 1, 1).start()
        self.x_copy().start()

    def begin_other(self):
        self.x_copy(True).wait_recv()
        self.copy(0, 1, 0).start()
        self.copy(1, 1, 0).start()

    def step(self, step):
        for mine in (1, 0):
            for way in (0, 1):
                self.copy(way, step, mine, True).wait_recv()
                if step < 3 or way == 1 - mine:
                    self.copy(way, step + 1, mine).start()

    def last(self):
        for mine in (1, 0):
            self.copy(1 - mine, 4, mine, True).wait_recv()

    def drain(self):
        self.x_copy().wait_send()
        for mine in (1, 0):
            for way in (0, 1):
                for step in range(1, 5 if way == 1 - mine else 4):
                    self.copy(way, step, mine).wait_send()


class HalfGather:
    def __init__(self, place, buf, send, recv):
        self.place, self.buf, self.send, self.recv = place, buf, send, recv

    def copy(self, way, step, half, arriving=False):
        place = self.place
        sign = 1 - 2 * way
        block = lax.rem(place.z - sign * (step if arriving else step - 1) + Z, Z)
        part = self.buf.at[block, half]
        at = (way, step - 1, half)
        return remote(part, part, self.send.at[at], self.recv.at[at], place.z_next[way])

    def begin(self, half):
        for way in (0, 1):
            self.copy(way, 1, half).start()

    def step(self, step):
        for half in (0, 1):
            for way in (0, 1):
                self.copy(way, step, half, True).wait_recv()
                if step < 3 or way == half:
                    self.copy(way, step + 1, half).start()

    def last(self, half):
        self.copy(half, 4, half, True).wait_recv()

    def drain(self, first=1):
        for half in (0, 1):
            for way in (0, 1):
                for step in range(first, 5 if way == half else 4):
                    self.copy(way, step, half).wait_send()


class Direct:
    def __init__(self, me, device_of, out, into, send, recv):
        self.me, self.device_of, self.out, self.into, self.send, self.recv = me, device_of, out, into, send, recv

    def copy(self, apart):
        peer = lax.rem(self.me + apart, 8)
        return remote(
            self.out(peer), self.into(self.me), self.send.at[apart - 1], self.recv.at[apart - 1], self.device_of(peer)
        )

    def start(self):
        for apart in (4, 3, 5, 2, 6, 1, 7):
            self.copy(apart).start()

    def wait_one(self, apart):
        source = lax.rem(self.me - apart + 8, 8)
        part = self.into(source)
        remote(part, part, self.send.at[apart - 1], self.recv.at[apart - 1], self.device_of(source)).wait_recv()

    def wait(self):
        for apart in (1, 7, 2, 6, 3, 5, 4):
            self.wait_one(apart)

    def drain(self):
        for apart in range(1, 8):
            self.copy(apart).wait_send()


class Total:
    def __init__(self, place, m, zs, x, x_got, r, r_got, m_s, m_r, z_s, z_r, one_s, one_r):
        self.place, self.m, self.zs, self.x, self.x_got, self.r, self.r_got = place, m, zs, x, x_got, r, r_got
        self.m_all = Direct(place.mp, place.of_mp, lambda peer: m.at[place.mp], lambda source: m.at[source], m_s, m_r)
        self.z_all = Direct(place.z, place.of_z, lambda peer: zs.at[place.z], lambda source: zs.at[source], z_s, z_r)
        self.one_s, self.one_r = one_s, one_r

    def x_copy(self):
        return remote(self.x, self.x_got, self.one_s.at[0], self.one_r.at[0], self.place.x_other)

    def r_copy(self):
        return remote(self.r, self.r_got, self.one_s.at[1], self.one_r.at[1], self.place.partner)

    def in_order(self, slots):
        total = slots[0]
        for source in range(1, 8):
            total = total + slots[source]
        return total

    def start(self, tile):
        self.m[self.place.mp] = tile
        self.m_all.start()

    def over_x(self):
        self.m_all.wait()
        self.x[...] = self.in_order(self.m)
        self.x_copy().start()

    def over_z(self):
        self.x_copy().wait_recv()
        self.zs[self.place.z] = self.x[...] + self.x_got[...]
        self.z_all.start()

    def over_role(self):
        self.z_all.wait()
        self.r[...] = self.in_order(self.zs)
        self.r_copy().start()

    def result(self):
        self.r_copy().wait_recv()
        return self.r[...] + self.r_got[...]

    def drain(self):
        self.m_all.drain()
        self.x_copy().wait_send()
        self.z_all.drain()
        self.r_copy().wait_send()


class Place:
    def __init__(self):
        self.role, self.mp, self.dp = lax.axis_index("role"), lax.axis_index("mp"), lax.axis_index("dp")
        dp = self.dp
        self.z, self.x = dp // 2, lax.rem(dp, 2)
        role, mp, z, x = self.role, self.mp, self.z, self.x
        up, down = lax.rem(z + 1, Z) * 2 + x, lax.rem(z + Z - 1, Z) * 2 + x
        self.z_next = ((role, up, mp), (role, down, mp))
        self.z_next_cross = ((1 - role, up, mp), (1 - role, down, mp))
        self.x_other = (role, z * 2 + 1 - x, mp)
        self.partner = (1 - role, dp, mp)
        self.across = (role, mp * 2 + x, z)
        self.of_z = lambda peer: (role, peer * 2 + x, mp)
        self.of_mp = lambda peer: (role, dp, peer)


def exchange_kernel(
    tok_in, w_in, down_in, lin_in,
    tok_out, cot_out, hid_out, err_out, lin_out, stat_out,
    tok, w, down, lin,
    part, b_out, b_into, bx_out, bx_into, pre, hid,
    d_part, d_out, d_into, err, target_out, target,
    lin_part, e_out, e_into, ex_out, ex_into, lin_err,
    k_out, k_into, kx_out, kx_into, gate_out, cot,
    m1, z1, x1, x1_got, r1, r1_got, m2, z2, x2, x2_got, r2, r2_got, stat,
    load_sem, store_sem,
    tok_s, tok_r, hand_s, hand_r, b_s, b_r, bx_s, bx_r, c_s, c_r,
    d_s, d_r, one_s, one_r, i_s, i_r, e_s, e_r, k_s, k_r,
    j_s, j_r, jx_s, jx_r, l_s, l_r, g_s, g_r, gn_s,
    m1_s, m1_r, z1_s, z1_r, o1_s, o1_r, m2_s, m2_r, z2_s, z2_r, o2_s, o2_r,
    share_s, share_r,
):
    place = Place()
    role, mp, dp, z, x = place.role, place.mp, place.dp, place.z, place.x
    student, teacher = role == 1, role == 0
    x_of = (1 - x, x)
    halves = (0, 1)

    loads = [
        pltpu.make_async_copy(tok_in.at[:, b * QUARTER : (b + 1) * QUARTER], tok.at[b, mp], load_sem.at[b])
        for b in halves
    ]
    loads += [
        pltpu.make_async_copy(w_in, w, load_sem.at[2]),
        pltpu.make_async_copy(down_in, down, load_sem.at[3]),
    ]
    loads += [
        pltpu.make_async_copy(
            lin_in.at[:, pl.ds(pl.multiple_of(b * 2 * QUARTER + role * QUARTER, QUARTER), QUARTER)],
            lin.at[b],
            load_sem.at[4 + b],
        )
        for b in halves
    ]
    for load in loads:
        load.start()

    barrier = pltpu.get_barrier_semaphore()

    def greet(device):
        pl.semaphore_signal(barrier, inc=1, device_id=device, device_id_type=MESH)

    for apart in range(1, 8):
        greet(place.of_mp(lax.rem(mp + apart, 8)))
        greet((1 - role, dp, lax.rem(mp + apart, 8)))
        greet(place.of_z(lax.rem(z + apart, 8)))
    greet(place.x_other)
    greet(place.partner)
    for way in (0, 1):
        greet(place.z_next_cross[way])

    @pl.when(z != mp)
    def _():
        greet(place.across)
        pl.semaphore_wait(barrier, 26)

    @pl.when(z == mp)
    def _():
        pl.semaphore_wait(barrier, 25)

    for load in loads[:2]:
        load.wait()
    tokens = Direct(mp, place.of_mp, lambda peer: tok.at[role, mp], lambda source: tok.at[role, source], tok_s, tok_r)
    tokens.start()

    def hand(apart, arriving=False):
        source = lax.rem(mp - apart + 8, 8)
        part_of = tok.at[1 - role if arriving else role, source]
        return remote(part_of, part_of, hand_s.at[apart - 1], hand_r.at[apart - 1], place.partner)

    for apart in (1, 7, 2, 6, 3, 5, 4):
        tokens.wait_one(apart)
        hand(apart).start()
    loads[2].wait()
    for apart in (1, 7, 2, 6, 3, 5, 4):
        hand(apart, True).wait_recv()
    stores = [pltpu.make_async_copy(tok, tok_out, store_sem.at[0])]
    stores[0].start()

    def all_tokens():
        return jnp.concatenate([tok[b].reshape(Z * ROWS, QUARTER) for b in halves], axis=1)

    tags = [(h, g) for h in halves for g in (0, 1)]
    b_sum = RingSum(place, part, b_out, b_into, b_s, b_r, tags, lambda tag: tag[1])
    for h, g in tags:
        column = g * UNITS + h * HALF
        part[h, g] = jnp.dot(
            all_tokens(), w[:, column : column + HALF], preferred_element_type=F32
        ).reshape(Z, ROWS, HALF)
        b_sum.begin((h, g))
    b_sum.step(2)
    for load in loads[3:]:
        load.wait()
    for q in (0, 1):
        lin_part[q] = jnp.dot(all_tokens(), lin[x_of[q]], preferred_element_type=F32).reshape(Z, ROWS, QUARTER)
    b_sum.step(3)
    b_sum.step(4)

    def bx_copy(h, g):
        return remote(bx_out.at[h, g], bx_into.at[h, g], bx_s.at[h, g], bx_r.at[h, g], place.x_other)

    for h, g in tags:
        bx_out[h, g] = b_sum.result((h, g)).astype(BF16)
        bx_copy(h, g).start()

    c_all = HalfGather(place, hid, c_s, c_r)
    for h in halves:
        for g in (0, 1):
            bx_copy(h, g).wait_recv()
            pre[h, g] = bx_out[h, g].astype(F32) + bx_into[h, g].astype(F32)
        gate = pre[h, 0]
        hid[z, h] = (gate * jax.nn.sigmoid(gate) * pre[h, 1]).astype(BF16)
        c_all.begin(h)
    e_sum = RingSum(place, lin_part, e_out, e_into, e_s, e_r, [(0,), (1,)], lambda tag: tag[0])
    for step in (1, 2, 3):
        c_all.step(step)
    for tag in e_sum.tags:
        e_sum.begin(tag)

    c_all.last(0)
    d_part[...] = jnp.dot(hid[:, 0].reshape(Z * ROWS, HALF), down[:HALF], preferred_element_type=F32)
    c_all.last(1)

    def d_copy(b, apart):
        peer = lax.rem(mp + apart, 8)
        return remote(
            d_out.at[b, peer], d_into.at[role, mp], d_s.at[b, apart - 1], d_r.at[role, apart - 1], (b, dp, peer)
        )

    def d_arrival(source_role, apart):
        source = lax.rem(mp - apart + 8, 8)
        got = d_into.at[source_role, source]
        return remote(got, got, d_s.at[0, apart - 1], d_r.at[source_role, apart - 1], (source_role, dp, source))

    def d_partner(arriving=False):
        return remote(
            d_out.at[1 - role, mp],
            d_into.at[1 - role if arriving else role, mp],
            one_s.at[0],
            one_r.at[0],
            place.partner,
        )

    for b in halves:
        columns = slice(b * QUARTER, (b + 1) * QUARTER)
        total = d_part[:, columns] + jnp.dot(
            hid[:, 1].reshape(Z * ROWS, HALF), down[HALF:, columns], preferred_element_type=F32
        )
        d_out[b] = total.reshape(Z, ROWS, QUARTER).astype(BF16)
        for apart in (4, 3, 5, 2, 6, 1, 7):
            d_copy(b, apart).start()
    d_partner().start()
    d_into[role, mp] = d_out[role, mp]
    e_sum.step(2)
    for apart in (1, 7, 2, 6, 3, 5, 4):
        for source_role in (0, 1):
            d_arrival(source_role, apart).wait_recv()
    d_partner(True).wait_recv()

    def summed(source_role):
        own = d_into[source_role, 0].astype(F32)
        for source in range(1, 8):
            own = own + d_into[source_role, source].astype(F32)
        return own.astype(BF16)

    teacher_rows = summed(0)
    error = summed(1).astype(F32) - teacher_rows.astype(F32)
    err[role, mp] = error.astype(BF16)

    def err_copy(apart):
        peer = lax.rem(mp + apart, 8)
        return remote(
            err.at[role, mp], err.at[role, mp], i_s.at[apart - 1], i_r.at[role, apart - 1], (1, dp, peer)
        )

    def err_arrival(source_role, apart):
        source = lax.rem(mp - apart + 8, 8)
        got = err.at[source_role, source]
        return remote(got, got, i_s.at[apart - 1], i_r.at[source_role, apart - 1], (source_role, dp, source))

    def err_partner():
        return remote(err.at[0, mp], err.at[0, mp], one_s.at[1], one_r.at[1], place.partner)

    for apart in (4, 3, 5, 2, 6, 1, 7):
        err_copy(apart).start()

    @pl.when(teacher)
    def _():
        err_partner().start()

    target_out[...] = teacher_rows

    def target_copy():
        return remote(target_out, target, one_s.at[2], one_r.at[2], place.across)

    @pl.when(z != mp)
    def _():
        target_copy().start()

    @pl.when(z == mp)
    def _():
        target[...] = target_out[...]

    row = lax.broadcasted_iota(jnp.int32, (8, 128), 0)
    teacher_float = teacher_rows.astype(F32)
    target_square = jnp.sum(teacher_float * teacher_float)
    error_square = jnp.sum(error * error)
    norm = Total(place, m1, z1, x1, x1_got, r1, r1_got, m1_s, m1_r, z1_s, z1_r, o1_s, o1_r)
    norm.start(jnp.where(row == 0, target_square, jnp.where(row == 1, error_square, 0.0)))
    e_sum.step(3)

    k_sum = RingSum(place, part.at[:, 0], k_out, k_into, k_s, k_r, [(0,), (1,)], lambda tag: tag[0])

    def err_share():
        return remote(err, err_out, share_s.at[2], share_r.at[2], place.partner)

    def err_store():
        return pltpu.make_async_copy(err, err_out, store_sem.at[3])

    def hid_share(h):
        return remote(
            hid.at[:, h], hid_out.at[:, :, h * HALF : (h + 1) * HALF], share_s.at[h], share_r.at[h], place.partner
        )

    def hid_store(h):
        return pltpu.make_async_copy(hid.at[:, h], hid_out.at[:, :, h * HALF : (h + 1) * HALF], store_sem.at[1 + h])

    @pl.when(student)
    def _():
        for apart in (1, 7, 2, 6, 3, 5, 4):
            for source_role in (0, 1):
                err_arrival(source_role, apart).wait_recv()
        err_partner().wait_recv()
        for h in halves:
            part[h, 0] = lax.dot_general(
                jnp.concatenate([err[b].reshape(Z * ROWS, QUARTER) for b in halves], axis=1),
                down[h * HALF : (h + 1) * HALF],
                (((1,), (1,)), ((), ())),
                preferred_element_type=F32,
            ).reshape(Z, ROWS, HALF)
            k_sum.begin((h,))
        err_share().start()
        err_store().start()
        for h in halves:
            hid_share(h).start()
            hid_store(h).start()

    norm.over_x()
    e_sum.step(4)
    norm.over_z()

    @pl.when(student)
    def _():
        k_sum.step(2)

    def ex_copy():
        return remote(ex_out, ex_into, one_s.at[3], one_r.at[3], place.x_other)

    ex_out[...] = e_sum.result((0,)).astype(BF16)
    ex_copy().start()
    linear_rows = e_sum.result((1,))
    norm.over_role()

    @pl.when(student)
    def _():
        k_sum.step(3)

    ex_copy().wait_recv()

    @pl.when(z != mp)
    def _():
        target_copy().wait_recv()

    linear_error = linear_rows + ex_into[...].astype(F32) - target[...].astype(F32)
    lin_err[z, x] = linear_error.astype(BF16)
    j_all = RingGather(place, lin_err, j_s, j_r, jx_s.at[0], jx_r.at[0])
    j_all.begin()
    loss = Total(place, m2, z2, x2, x2_got, r2, r2_got, m2_s, m2_r, z2_s, z2_r, o2_s, o2_r)
    loss.start(jnp.where(row == 2, jnp.sum(linear_error * linear_error), 0.0))

    @pl.when(student)
    def _():
        k_sum.step(4)

    stat[...] = norm.result()
    j_all.begin_other()
    loss.over_x()

    def kx_copy(h):
        return remote(kx_out.at[h], kx_into.at[h], bx_s.at[2, h], bx_r.at[2, h], place.x_other)

    def gate_copy(h):
        return remote(gate_out.at[h], cot.at[z, h], g_s.at[h], g_r.at[h], place.partner)

    l_all = HalfGather(place, cot, l_s, l_r)

    def gate_next(way, h):
        return remote(
            gate_out.at[h], cot.at[z, h], gn_s.at[way, h], l_r.at[way, 0, h], place.z_next_cross[way]
        )

    @pl.when(student)
    def _():
        for h in halves:
            kx_out[h] = k_sum.result((h,)).astype(BF16)
            kx_copy(h).start()
        factor = (16.0 * MODEL) / stat[0:1, 0:1]
        for h in halves:
            kx_copy(h).wait_recv()
            hidden_cot = (kx_out[h].astype(F32) + kx_into[h].astype(F32)) * factor
            gate_pre, up_pre = pre[h, 0], pre[h, 1]
            sig = jax.nn.sigmoid(gate_pre)
            gate_out[h] = (hidden_cot * up_pre * sig * (1.0 + gate_pre * (1.0 - sig))).astype(BF16)
            for way in (0, 1):
                gate_next(way, h).start()
            cot[z, h] = (hidden_cot * gate_pre * sig).astype(BF16)
            l_all.begin(h)
            gate_copy(h).start()

    j_all.step(1)
    loss.over_z()
    l_all.step(1)
    j_all.step(2)
    loss.over_role()
    l_all.step(2)
    j_all.step(3)
    stat[...] = stat[...] + loss.result()
    stores.append(pltpu.make_async_copy(stat, stat_out, store_sem.at[4]))
    stores[-1].start()
    l_all.step(3)
    j_all.last()

    def lin_columns(b):
        start = pl.multiple_of(b * 2 * QUARTER + role * QUARTER, QUARTER)
        return lin_out.at[:, :, pl.ds(start, QUARTER)]

    def lin_share(b):
        return remote(lin_err.at[:, b], lin_columns(b), share_s.at[3 + b], share_r.at[3 + b], place.partner)

    def lin_arrival(b):
        start = pl.multiple_of(b * 2 * QUARTER + (1 - role) * QUARTER, QUARTER)
        got = lin_out.at[:, :, pl.ds(start, QUARTER)]
        return remote(lin_err.at[:, b], got, share_s.at[3 + b], share_r.at[3 + b], place.partner)

    for b in halves:
        lin_share(b).start()
        stores.append(pltpu.make_async_copy(lin_err.at[:, b], lin_columns(b), store_sem.at[5 + b]))
        stores[-1].start()

    @pl.when(teacher)
    def _():
        for h in halves:
            gate_copy(h).wait_recv()

    for h in halves:
        l_all.last(h)
        stores.append(
            pltpu.make_async_copy(cot.at[:, h], cot_out.at[:, :, h * HALF : (h + 1) * HALF], store_sem.at[7 + h])
        )
        stores[-1].start()

    tokens.drain()
    for apart in range(1, 8):
        hand(apart).wait_send()
        err_copy(apart).wait_send()
        for b in halves:
            d_copy(b, apart).wait_send()
    d_partner().wait_send()
    b_sum.drain()
    for h, g in tags:
        bx_copy(h, g).wait_send()
    c_all.drain()
    e_sum.drain()
    ex_copy().wait_send()
    norm.drain()
    loss.drain()
    j_all.drain()
    for b in halves:
        lin_share(b).wait_send()

    @pl.when(z != mp)
    def _():
        target_copy().wait_send()

    @pl.when(student)
    def _():
        k_sum.drain()
        l_all.drain()
        err_share().wait_send()
        err_store().wait()
        for h in halves:
            kx_copy(h).wait_send()
            gate_copy(h).wait_send()
            for way in (0, 1):
                gate_next(way, h).wait_send()
            hid_share(h).wait_send()
            hid_store(h).wait()

    @pl.when(teacher)
    def _():
        l_all.drain(2)
        err_partner().wait_send()
        err_share().wait_recv()
        for h in halves:
            hid_share(h).wait_recv()

    for b in halves:
        lin_arrival(b).wait_recv()
    for store in stores:
        store.wait()


def exchange(tokens, w, down, linear):
    def vmem(*shape, dtype=BF16):
        return pltpu.VMEM(shape, dtype)

    def sems(*shape):
        return pltpu.SemaphoreType.DMA(shape)

    def array(*shape, dtype=BF16):
        return jax.ShapeDtypeStruct(shape, dtype)

    def total_tiles():
        return [vmem(8, 8, 128, dtype=F32)] * 2 + [vmem(8, 128, dtype=F32)] * 4

    anywhere = pl.BlockSpec(memory_space=pl.ANY)
    return pl.pallas_call(
        exchange_kernel,
        out_shape=[
            array(2, Z, ROWS, QUARTER),
            array(Z, ROWS, UNITS),
            array(Z, ROWS, UNITS),
            array(2, Z, ROWS, QUARTER),
            array(Z, ROWS, LIN),
            array(8, 128, dtype=F32),
        ],
        in_specs=[anywhere] * 4,
        out_specs=[anywhere] * 6,
        scratch_shapes=[
            vmem(2, Z, ROWS, QUARTER), vmem(WIDTH, 2 * UNITS), vmem(UNITS, WIDTH), vmem(2, WIDTH, QUARTER),
            vmem(2, 2, Z, ROWS, HALF, dtype=F32), vmem(2, 4, 2, 2, ROWS, HALF), vmem(2, 4, 2, 2, ROWS, HALF),
            vmem(2, 2, ROWS, HALF), vmem(2, 2, ROWS, HALF), vmem(2, 2, ROWS, HALF, dtype=F32), vmem(Z, 2, ROWS, HALF),
            vmem(Z * ROWS, WIDTH, dtype=F32), vmem(2, 8, ROWS, QUARTER), vmem(2, 8, ROWS, QUARTER),
            vmem(2, 8, ROWS, QUARTER), vmem(ROWS, QUARTER), vmem(ROWS, QUARTER),
            vmem(2, Z, ROWS, QUARTER, dtype=F32), vmem(2, 4, 2, ROWS, QUARTER), vmem(2, 4, 2, ROWS, QUARTER),
            vmem(ROWS, QUARTER), vmem(ROWS, QUARTER), vmem(Z, 2, ROWS, QUARTER),
            vmem(2, 4, 2, ROWS, HALF), vmem(2, 4, 2, ROWS, HALF), vmem(2, ROWS, HALF), vmem(2, ROWS, HALF),
            vmem(2, ROWS, HALF), vmem(Z, 2, ROWS, HALF),
            *total_tiles(), *total_tiles(), vmem(8, 128, dtype=F32),
            sems(6), sems(9),
            sems(7), sems(7), sems(7), sems(7), sems(2, 4, 2, 2), sems(2, 4, 2, 2), sems(3, 2), sems(3, 2),
            sems(2, 4, 2), sems(2, 4, 2),
            sems(2, 7), sems(2, 7), sems(4), sems(4), sems(7), sems(2, 7), sems(2, 4, 2), sems(2, 4, 2),
            sems(2, 4, 2), sems(2, 4, 2),
            sems(2, 4, 2), sems(2, 4, 2), sems(1), sems(1), sems(2, 4, 2), sems(2, 4, 2), sems(2), sems(2), sems(2, 2),
            sems(7), sems(7), sems(7), sems(7), sems(2), sems(2),
            sems(7), sems(7), sems(7), sems(7), sems(2), sems(2),
            sems(5), sems(5),
        ],
        compiler_params=pltpu.CompilerParams(
            collective_id=0, has_side_effects=True, vmem_limit_bytes=34 * 1024 * 1024
        ),
        name="exchange",
    )(tokens, w, down, linear)


def contract_rows(left, right):
    return lax.dot_general(left, right, (((0,), (0,)), ((), ())), preferred_element_type=F32)


BLOCK = 256


def gradients_kernel(tok, cot, hid, err, lin_err, stat, unit_grad, down_grad, linear_grad, losses, turned):
    step = pl.program_id(0)
    factor = (16.0 * MODEL) / stat[0:1, 0:1]

    @pl.when(step == 0)
    def _():
        for b in (0, 1):
            turned[b * QUARTER : (b + 1) * QUARTER] = tok[b].T
        share = stat[...] / stat[0:1, 0:1]
        losses[0] = share[1, 0]
        losses[1] = share[2, 0]

    unit_grad[...] = jnp.dot(turned[...], cot[...], preferred_element_type=F32).astype(BF16)
    for b in (0, 1):
        down_grad[:, b * QUARTER : (b + 1) * QUARTER] = (factor * contract_rows(hid[...], err[b])).astype(BF16)

    @pl.when(step < LIN // BLOCK)
    def _():
        linear_grad[...] = (factor * jnp.dot(turned[...], lin_err[...], preferred_element_type=F32)).astype(BF16)


def gradients(tok, cot, hid, err, lin_err, stat):
    tokens = Z * ROWS
    last = LIN // BLOCK - 1
    halves = pl.BlockSpec((2, tokens, QUARTER), lambda i: (0, 0, 0))
    return pl.pallas_call(
        gradients_kernel,
        grid=(UNITS // BLOCK,),
        out_shape=[
            jax.ShapeDtypeStruct((WIDTH, UNITS), BF16),
            jax.ShapeDtypeStruct((UNITS, WIDTH), BF16),
            jax.ShapeDtypeStruct((WIDTH, LIN), BF16),
            jax.ShapeDtypeStruct((2,), F32),
        ],
        in_specs=[
            halves,
            pl.BlockSpec((tokens, BLOCK), lambda i: (0, i)),
            pl.BlockSpec((tokens, BLOCK), lambda i: (0, i)),
            halves,
            pl.BlockSpec((tokens, BLOCK), lambda i: (0, jnp.minimum(i, last))),
            pl.BlockSpec((8, 128), lambda i: (0, 0)),
        ],
        out_specs=[
            pl.BlockSpec((WIDTH, BLOCK), lambda i: (0, i)),
            pl.BlockSpec((BLOCK, WIDTH), lambda i: (i, 0)),
            pl.BlockSpec((WIDTH, BLOCK), lambda i: (0, jnp.minimum(i, last))),
            pl.BlockSpec(memory_space=pltpu.SMEM),
        ],
        scratch_shapes=[pltpu.VMEM((WIDTH, tokens), BF16)],
        compiler_params=pltpu.CompilerParams(vmem_limit_bytes=16 * 1024 * 1024),
        name="gradients",
    )(tok, cot, hid, err, lin_err, stat)


def body(tokens, gate_up, down, linear):
    w = gate_up.reshape(WIDTH, 2 * UNITS)
    tok, cot, hid, err, lin_err, stat = exchange(tokens, w, down[0], linear)
    rows = Z * ROWS
    unit_grad, down_grad, linear_grad, losses = gradients(
        tok.reshape(2, rows, QUARTER),
        cot.reshape(rows, UNITS),
        hid.reshape(rows, UNITS),
        err.reshape(2, rows, QUARTER),
        lin_err.reshape(rows, LIN),
        stat,
    )
    return (unit_grad[None], down_grad, linear_grad, losses)


def solution(mesh):
    return jax.shard_map(
        body,
        mesh=mesh,
        in_specs=(P("mp", "dp"), P("role", "dp", None, "mp"), P("role", "mp", "dp"), P("dp", "mp")),
        out_specs=(P("role", "dp", "mp"), P("mp", "dp"), P("dp", "mp"), P()),
        check_vma=False,
    )
```

time: 146 us -> 133 us (0.911)
  matrix products: 7.97 us -> 0 us
  between operations: 4 us -> 0.68 us
  Pallas kernels: 127 us -> 130 us
  local copies, waits for them, and re-layouts: 5.75 us -> 2.84 us
    dot_general x3 -> x0, matrix products: 7.97 us -> none  [contract_rows(): lax.dot_general(left, right, (((0,), (0,)), ((), ())), preferred_element_...]
    pallas_call x1 -> x2, Pallas kernels: 127 us -> 130 us  [the longest x1 123 us: exchange(): pl.pallas_call(exchange_kernel, out_shape=[array(2, Z, ROWS, QUARTER), ar...]
    unnamed x7, local copies, waits for them, and re-layouts: 4.44 us -> 2.84 us
where the time goes in v2:
time: 133 us
  Pallas kernels  130 us (98%)
  local copies, waits for them, and re-layouts  2.84 us (2%)
    pallas_call x1, Pallas kernels, exchange(): pl.pallas_call(exchange_kernel, out_shape=[array(2, Z, ROWS, QUARTER), ar...  123 us
    pallas_call x1, Pallas kernels, gradients(): pl.pallas_call(gradients_kernel, grid=(UNITS // BLOCK,), out_shape=[jax.S...  6.27 us
    unnamed x7, local copies, waits for them, and re-layouts  2.84 us

profile of v2, /device:TPU:1, one launch (start us, length us, event | category | flops | bytes accessed | tf_op | source)
XLA Modules:
  0.0 133.2 jit_solution(4187074511535878344)
XLA Ops:
  0.6 0.0 copy-start
  0.6 0.0 copy-start.1
  0.7 0.0 copy-start.2
  0.7 2.8 %copy.8 = bf16[64,8,2,1792]{3,1,2,0:T(8,128)(2,1)S(1)} copy(bf16[64,8,2,1792]{3,2,1,0:T(2,128)(2,1)} %bitcast.17) | data formatting | bytes 7340032
  3.4 0.0 copy-done
  3.5 0.1 copy-done.1
  3.5 0.0 copy-done.2
  3.5 123.5 %exchange.1 = (bf16[2,8,48,256]{3,2,1,0:T(8,128)(2,1)S(1)}, bf16[8,48,1792]{2,1,0:T(8,128)(2,1)S(1)}, bf16[8,48,1792]{2,1,0:T(8,128)(2,1)S(1)}, bf16[2,8,48,256]...) custom-call(bf16[48,512]{1,0:T(8,128)(2,1)S(1)} %copy-done.2, ...), custom_call_target="tpu_custom_call" | custom-call | tf_op jit(solution)/shard_map/exchange/pallas_call | solution.py:676
  127.0 6.3 %gradients.1 = (bf16[512,1792]{1,0:T(8,128)(2,1)}, bf16[1792,512]{1,0:T(8,128)(2,1)}, bf16[512,1024]{1,0:T(8,128)(2,1)}, f32[2]{0:T(128)}) custom-call(bf16[2,384,256]{2,1,0:T(8,128)(2,1)S(1)} %bitcast.15, bf16[384,1792]{1,0:T(8,128)(2,1)S(1)} %bitcast.12, bf16[384,1792]{1,0:T(8,128)(2,1)S(1)} %bitcast.13, bf16[2,384,256]{2,1,0:T(8,128)(2,1)S(1)} %bitcast.16, ...), custom_call_target="tpu_custom_call" | custom-call | tf_op jit(solution)/shard_map/gradients/pallas_call | solution.py:748
Async XLA Ops:
  0.6 2.8 %copy-start = (bf16[1,1792,512]{2,1,0:T(8,128)(2,1)S(1)}, bf16[1,1792,512]{2,1,0:T(8,128)(2,1)}, u32[]{:S(2)}) copy-start(bf16[1,1792,512]{2,1,0:T(8,128)(2,1)} %param.6) | copy-start | bytes 5505028
  0.6 2.9 %copy-start.1 = (bf16[512,1024]{1,0:T(8,128)(2,1)S(1)}, bf16[512,1024]{1,0:T(8,128)(2,1)}, u32[]{:S(2)}) copy-start(bf16[512,1024]{1,0:T(8,128)(2,1)} %lin_in.1) | copy-start | bytes 3145732
  0.7 2.9 %copy-start.2 = (bf16[48,512]{1,0:T(8,128)(2,1)S(1)}, bf16[48,512]{1,0:T(8,128)(2,1)}, u32[]{:S(2)}) copy-start(bf16[48,512]{1,0:T(8,128)(2,1)} %tok_in.1) | copy-start | bytes 147460

commit v3 on v2

--- a/solution.py
+++ b/solution.py
@@ -12,7 +12,8 @@
 ROWS = 48
 WIDTH = 512
 UNITS = 1792
-HALF = UNITS // 2
+WHOLE = 1024
+SPLIT = 384
 LIN = 1024
 QUARTER = LIN // 4
 
@@ -36,14 +37,16 @@
 
     def push(self, way, step, tag, first):
         sign = 1 - 2 * way
-        block = lax.rem(self.place.z + sign * (5 - step) + Z, Z)
-        total = self.part[tag + (block,)]
+        total = self.local(tag, sign * (5 - step))
         if not first:
             self.copy(way, step - 1, tag).wait_recv()
             total = total + self.into[(way, step - 2) + tag].astype(F32)
         self.out[(way, step - 1) + tag] = total.astype(BF16)
         self.copy(way, step, tag).start()
 
+    def local(self, tag, offset):
+        return self.part[tag + (lax.rem(self.place.z + offset + Z, Z),)]
+
     def begin(self, tag):
         far = self.long_way(tag)
         self.push(far, 1, tag, True)
@@ -56,7 +59,7 @@
                     self.push(way, step, tag, False)
 
     def result(self, tag):
-        total = self.part[tag + (self.place.z,)]
+        total = self.local(tag, 0)
         for way in (0, 1):
             self.copy(way, 4, tag).wait_recv()
             total = total + self.into[(way, 3) + tag].astype(F32)
@@ -117,37 +120,109 @@
                     self.copy(way, step, mine).wait_send()
 
 
-class HalfGather:
-    def __init__(self, place, buf, send, recv):
-        self.place, self.buf, self.send, self.recv = place, buf, send, recv
-
-    def copy(self, way, step, half, arriving=False):
-        place = self.place
-        sign = 1 - 2 * way
-        block = lax.rem(place.z - sign * (step if arriving else step - 1) + Z, Z)
-        part = self.buf.at[block, half]
-        at = (way, step - 1, half)
-        return remote(part, part, self.send.at[at], self.recv.at[at], place.z_next[way])
-
-    def begin(self, half):
+class PairRingSum(RingSum):
+    def pair(self, other, x_out, x_into, x_send, x_recv):
+        self.other, self.x_out, self.x_into, self.x_send, self.x_recv = other, x_out, x_into, x_send, x_recv
+        self.got = set()
+
+    def block(self, offset):
+        return lax.rem(self.place.z + offset, Z)
+
+    def x_copy(self, offset):
+        block = self.block(offset)
+        return remote(
+            self.x_out.at[block], self.x_into.at[block], self.x_send.at[offset], self.x_recv.at[offset], self.place.x_other
+        )
+
+    def exchange(self):
+        for offset in (4, 3, 5, 2, 6, 1, 7, 0):
+            block = self.block(offset)
+            for tag in self.tags:
+                self.x_out[(block,) + tag] = self.other[tag + (block,)].astype(BF16)
+            self.x_copy(offset).start()
+
+    def local(self, tag, offset):
+        offset = offset % Z
+        if offset not in self.got:
+            self.got.add(offset)
+            self.x_copy(offset).wait_recv()
+        block = self.block(offset)
+        return self.part[tag + (block,)] + self.x_into[(block,) + tag].astype(F32)
+
+    def drain(self):
+        super().drain()
+        for offset in range(Z):
+            self.x_copy(offset).wait_send()
+
+
+class Gather:
+    def __init__(self, place, whole, split, w_send, w_recv, s_send, s_recv, x_send, x_recv):
+        self.place, self.whole, self.split = place, whole, split
+        self.w_send, self.w_recv, self.s_send, self.s_recv = w_send, w_recv, s_send, s_recv
+        self.x_send, self.x_recv = x_send, x_recv
+
+    def block(self, way, steps):
+        return lax.rem(self.place.z - (1 - 2 * way) * steps + Z, Z)
+
+    def w_copy(self, way, step, arriving=False):
+        part = self.whole.at[self.block(way, step if arriving else step - 1)]
+        if step == 4:
+            part = part.at[:, way * WHOLE // 2 : (way + 1) * WHOLE // 2]
+        at = (way, step - 1)
+        return remote(part, part, self.w_send.at[at], self.w_recv.at[at], self.place.z_next[way])
+
+    def s_copy(self, way, step, arriving=False):
+        part = self.split.at[self.block(way, step if arriving else step - 1), self.place.x]
+        at = (way, step - 1)
+        return remote(part, part, self.s_send.at[at], self.s_recv.at[at], self.place.z_next[way])
+
+    def x_copy(self, way, steps, arriving=False):
+        part = self.split.at[self.block(way, steps), 1 - self.place.x if arriving else self.place.x]
+        at = steps + 3 * way if steps else 0
+        return remote(part, part, self.x_send.at[at], self.x_recv.at[at], self.place.x_other)
+
+    def begin_split(self):
         for way in (0, 1):
-            self.copy(way, 1, half).start()
+            self.s_copy(way, 1).start()
+        self.x_copy(0, 0).start()
+
+    def begin_whole(self):
+        for way in (0, 1):
+            self.w_copy(way, 1).start()
 
     def step(self, step):
-        for half in (0, 1):
-            for way in (0, 1):
-                self.copy(way, step, half, True).wait_recv()
-                if step < 3 or way == half:
-                    self.copy(way, step + 1, half).start()
-
-    def last(self, half):
-        self.copy(half, 4, half, True).wait_recv()
+        for way in (0, 1):
+            self.s_copy(way, step, True).wait_recv()
+            if step < 3 or way == 1:
+                self.s_copy(way, step + 1).start()
+            self.x_copy(way, step).start()
+        for way in (0, 1):
+            self.w_copy(way, step, True).wait_recv()
+            self.w_copy(way, step + 1).start()
+
+    def last_split(self):
+        self.s_copy(1, 4, True).wait_recv()
+        self.x_copy(1, 4).start()
+
+    def last_whole(self):
+        for way in (0, 1):
+            self.w_copy(way, 4, True).wait_recv()
+
+    def crossings(self):
+        return [(0, 0)] + [(way, steps) for steps in (1, 2, 3) for way in (0, 1)] + [(1, 4)]
+
+    def wait_pair(self):
+        for way, steps in self.crossings():
+            self.x_copy(way, steps, True).wait_recv()
 
     def drain(self, first=1):
-        for half in (0, 1):
-            for way in (0, 1):
-                for step in range(first, 5 if way == half else 4):
-                    self.copy(way, step, half).wait_send()
+        for way in (0, 1):
+            for step in range(first, 5):
+                self.w_copy(way, step).wait_send()
+                if step < 4 or way == 1:
+                    self.s_copy(way, step).wait_send()
+        for way, steps in self.crossings():
+            self.x_copy(way, steps).wait_send()
 
 
 class Direct:
@@ -248,14 +323,17 @@
     tok_out, cot_out, hid_out, err_out, lin_out, stat_out,
     tok, w, down, lin,
     part, b_out, b_into, bx_out, bx_into, pre, hid,
+    s_part, s_out, s_into, sx_out, sx_into, s_pre, s_hid,
     d_part, d_out, d_into, err, target_out, target,
     lin_part, e_out, e_into, ex_out, ex_into, lin_err,
     k_out, k_into, kx_out, kx_into, gate_out, cot,
+    ks_out, ks_into, ksx_out, ksx_into, s_gate_out, s_cot,
     m1, z1, x1, x1_got, r1, r1_got, m2, z2, x2, x2_got, r2, r2_got, stat,
     load_sem, store_sem,
-    tok_s, tok_r, hand_s, hand_r, b_s, b_r, bx_s, bx_r, c_s, c_r,
-    d_s, d_r, one_s, one_r, i_s, i_r, e_s, e_r, k_s, k_r,
-    j_s, j_r, jx_s, jx_r, l_s, l_r, g_s, g_r, gn_s,
+    tok_s, tok_r, hand_s, hand_r, b_s, b_r, bx_s, bx_r, s_s, s_r, sx_s, sx_r,
+    c_s, c_r, cs_s, cs_r, cx_s, cx_r,
+    d_s, d_r, one_s, one_r, i_s, i_r, e_s, e_r, k_s, k_r, ks_s, ks_r, ksx_s, ksx_r,
+    j_s, j_r, jx_s, jx_r, l_s, l_r, ls_s, ls_r, lx_s, lx_r, g_s, g_r, gn_s,
     m1_s, m1_r, z1_s, z1_r, o1_s, o1_r, m2_s, m2_r, z2_s, z2_r, o2_s, o2_r,
     share_s, share_r,
 ):
@@ -329,46 +407,68 @@
     def all_tokens():
         return jnp.concatenate([tok[b].reshape(Z * ROWS, QUARTER) for b in halves], axis=1)
 
-    tags = [(h, g) for h in halves for g in (0, 1)]
-    b_sum = RingSum(place, part, b_out, b_into, b_s, b_r, tags, lambda tag: tag[1])
-    for h, g in tags:
-        column = g * UNITS + h * HALF
-        part[h, g] = jnp.dot(
-            all_tokens(), w[:, column : column + HALF], preferred_element_type=F32
-        ).reshape(Z, ROWS, HALF)
-        b_sum.begin((h, g))
+    tags = [(0,), (1,)]
+    b_sum = RingSum(place, part, b_out, b_into, b_s, b_r, tags, lambda tag: tag[0])
+    s_sum = PairRingSum(place, s_part.at[1], s_out, s_into, s_s, s_r, tags, lambda tag: tag[0])
+    s_sum.pair(s_part.at[0], sx_out, sx_into, sx_s, sx_r)
+
+    def split_dot(q):
+        for g in (0, 1):
+            column = pl.multiple_of(g * UNITS + WHOLE + x_of[q] * SPLIT, 128)
+            s_part[q, g] = jnp.dot(
+                all_tokens(), w[:, pl.ds(column, SPLIT)], preferred_element_type=F32
+            ).reshape(Z, ROWS, SPLIT)
+
+    split_dot(0)
+    s_sum.exchange()
+    for g in (0, 1):
+        part[g] = jnp.dot(
+            all_tokens(), w[:, g * UNITS : g * UNITS + WHOLE], preferred_element_type=F32
+        ).reshape(Z, ROWS, WHOLE)
+        b_sum.begin((g,))
+    split_dot(1)
+    for tag in tags:
+        s_sum.begin(tag)
     b_sum.step(2)
+    s_sum.step(2)
     for load in loads[3:]:
         load.wait()
     for q in (0, 1):
         lin_part[q] = jnp.dot(all_tokens(), lin[x_of[q]], preferred_element_type=F32).reshape(Z, ROWS, QUARTER)
-    b_sum.step(3)
-    b_sum.step(4)
-
-    def bx_copy(h, g):
-        return remote(bx_out.at[h, g], bx_into.at[h, g], bx_s.at[h, g], bx_r.at[h, g], place.x_other)
-
-    for h, g in tags:
-        bx_out[h, g] = b_sum.result((h, g)).astype(BF16)
-        bx_copy(h, g).start()
-
-    c_all = HalfGather(place, hid, c_s, c_r)
-    for h in halves:
-        for g in (0, 1):
-            bx_copy(h, g).wait_recv()
-            pre[h, g] = bx_out[h, g].astype(F32) + bx_into[h, g].astype(F32)
-        gate = pre[h, 0]
-        hid[z, h] = (gate * jax.nn.sigmoid(gate) * pre[h, 1]).astype(BF16)
-        c_all.begin(h)
+    for step in (3, 4):
+        b_sum.step(step)
+        s_sum.step(step)
+
+    def bx_copy(g):
+        return remote(bx_out.at[g], bx_into.at[g], bx_s.at[g], bx_r.at[g], place.x_other)
+
+    for g in (0, 1):
+        bx_out[g] = b_sum.result((g,)).astype(BF16)
+        bx_copy(g).start()
+
+    def hidden(inputs):
+        return (inputs[0] * jax.nn.sigmoid(inputs[0]) * inputs[1]).astype(BF16)
+
+    c_all = Gather(place, hid, s_hid, c_s, c_r, cs_s, cs_r, cx_s, cx_r)
+    for g in (0, 1):
+        s_pre[g] = s_sum.result((g,))
+    s_hid[z, x] = hidden(s_pre)
+    c_all.begin_split()
+    for g in (0, 1):
+        bx_copy(g).wait_recv()
+        pre[g] = bx_out[g].astype(F32) + bx_into[g].astype(F32)
+    hid[z] = hidden(pre)
+    c_all.begin_whole()
     e_sum = RingSum(place, lin_part, e_out, e_into, e_s, e_r, [(0,), (1,)], lambda tag: tag[0])
     for step in (1, 2, 3):
         c_all.step(step)
     for tag in e_sum.tags:
         e_sum.begin(tag)
 
-    c_all.last(0)
-    d_part[...] = jnp.dot(hid[:, 0].reshape(Z * ROWS, HALF), down[:HALF], preferred_element_type=F32)
-    c_all.last(1)
+    c_all.last_split()
+    c_all.last_whole()
+    d_part[...] = jnp.dot(hid[...].reshape(Z * ROWS, WHOLE), down[:WHOLE], preferred_element_type=F32)
+    c_all.wait_pair()
 
     def d_copy(b, apart):
         peer = lax.rem(mp + apart, 8)
@@ -393,7 +493,9 @@
     for b in halves:
         columns = slice(b * QUARTER, (b + 1) * QUARTER)
         total = d_part[:, columns] + jnp.dot(
-            hid[:, 1].reshape(Z * ROWS, HALF), down[HALF:, columns], preferred_element_type=F32
+            jnp.concatenate([s_hid[:, c].reshape(Z * ROWS, SPLIT) for c in halves], axis=1),
+            down[WHOLE:, columns],
+            preferred_element_type=F32,
         )
         d_out[b] = total.reshape(Z, ROWS, QUARTER).astype(BF16)
         for apart in (4, 3, 5, 2, 6, 1, 7):
@@ -458,7 +560,9 @@
     norm.start(jnp.where(row == 0, target_square, jnp.where(row == 1, error_square, 0.0)))
     e_sum.step(3)
 
-    k_sum = RingSum(place, part.at[:, 0], k_out, k_into, k_s, k_r, [(0,), (1,)], lambda tag: tag[0])
+    k_sum = RingSum(place, part.at[0], k_out, k_into, k_s, k_r, [()], lambda tag: 0)
+    ks_sum = PairRingSum(place, s_part.at[1, 0], ks_out, ks_into, ks_s, ks_r, [()], lambda tag: 1)
+    ks_sum.pair(s_part.at[0, 0], ksx_out, ksx_into, ksx_s, ksx_r)
 
     def err_share():
         return remote(err, err_out, share_s.at[2], share_r.at[2], place.partner)
@@ -466,13 +570,30 @@
     def err_store():
         return pltpu.make_async_copy(err, err_out, store_sem.at[3])
 
-    def hid_share(h):
-        return remote(
-            hid.at[:, h], hid_out.at[:, :, h * HALF : (h + 1) * HALF], share_s.at[h], share_r.at[h], place.partner
-        )
-
-    def hid_store(h):
-        return pltpu.make_async_copy(hid.at[:, h], hid_out.at[:, :, h * HALF : (h + 1) * HALF], store_sem.at[1 + h])
+    def parts_of(whole, split, out):
+        yield whole, out.at[:, :, :WHOLE]
+        for b in halves:
+            yield split.at[:, b], out.at[:, :, WHOLE + b * SPLIT : WHOLE + (b + 1) * SPLIT]
+
+    def hid_shares():
+        return [
+            remote(here, there, share_s.at[5 + i], share_r.at[5 + i], place.partner)
+            for i, (here, there) in enumerate(parts_of(hid, s_hid, hid_out))
+        ]
+
+    def hid_stores():
+        return [
+            pltpu.make_async_copy(here, there, store_sem.at[7 + i])
+            for i, (here, there) in enumerate(parts_of(hid, s_hid, hid_out))
+        ]
+
+    def cot_dot(start, size):
+        return lax.dot_general(
+            jnp.concatenate([err[b].reshape(Z * ROWS, QUARTER) for b in halves], axis=1),
+            down[pl.ds(start, size)],
+            (((1,), (1,)), ((), ())),
+            preferred_element_type=F32,
+        ).reshape(Z, ROWS, size)
 
     @pl.when(student)
     def _():
@@ -480,19 +601,16 @@
             for source_role in (0, 1):
                 err_arrival(source_role, apart).wait_recv()
         err_partner().wait_recv()
-        for h in halves:
-            part[h, 0] = lax.dot_general(
-                jnp.concatenate([err[b].reshape(Z * ROWS, QUARTER) for b in halves], axis=1),
-                down[h * HALF : (h + 1) * HALF],
-                (((1,), (1,)), ((), ())),
-                preferred_element_type=F32,
-            ).reshape(Z, ROWS, HALF)
-            k_sum.begin((h,))
+        s_part[0, 0] = cot_dot(pl.multiple_of(WHOLE + x_of[0] * SPLIT, 128), SPLIT)
+        ks_sum.exchange()
+        part[0] = cot_dot(0, WHOLE)
+        k_sum.begin(())
+        s_part[1, 0] = cot_dot(pl.multiple_of(WHOLE + x_of[1] * SPLIT, 128), SPLIT)
+        ks_sum.begin(())
         err_share().start()
         err_store().start()
-        for h in halves:
-            hid_share(h).start()
-            hid_store(h).start()
+        for copy in hid_shares() + hid_stores():
+            copy.start()
 
     norm.over_x()
     e_sum.step(4)
@@ -501,6 +619,7 @@
     @pl.when(student)
     def _():
         k_sum.step(2)
+        ks_sum.step(2)
 
     def ex_copy():
         return remote(ex_out, ex_into, one_s.at[3], one_r.at[3], place.x_other)
@@ -513,6 +632,7 @@
     @pl.when(student)
     def _():
         k_sum.step(3)
+        ks_sum.step(3)
 
     ex_copy().wait_recv()
 
@@ -530,49 +650,82 @@
     @pl.when(student)
     def _():
         k_sum.step(4)
+        ks_sum.step(4)
 
     stat[...] = norm.result()
     j_all.begin_other()
+
+    def kx_copy():
+        return remote(kx_out, kx_into, bx_s.at[2], bx_r.at[2], place.x_other)
+
+    def gate_copies():
+        return [
+            remote(s_gate_out, s_cot.at[z, x], g_s.at[0], g_r.at[0], place.partner),
+            remote(gate_out, cot.at[z], g_s.at[1], g_r.at[1], place.partner),
+        ]
+
+    l_all = Gather(place, cot, s_cot, l_s, l_r, ls_s, ls_r, lx_s, lx_r)
+
+    def gate_next(way):
+        return [
+            remote(s_gate_out, s_cot.at[z, x], gn_s.at[way, 0], ls_r.at[way, 0], place.z_next_cross[way]),
+            remote(gate_out, cot.at[z], gn_s.at[way, 1], l_r.at[way, 0], place.z_next_cross[way]),
+        ]
+
+    def cotangents(total, inputs):
+        factor = (16.0 * MODEL) / stat[0:1, 0:1]
+        hidden_cot = total * factor
+        gate_pre, up_pre = inputs[0], inputs[1]
+        sig = jax.nn.sigmoid(gate_pre)
+        gate_cot = hidden_cot * up_pre * sig * (1.0 + gate_pre * (1.0 - sig))
+        return gate_cot.astype(BF16), (hidden_cot * gate_pre * sig).astype(BF16)
+
+    @pl.when(student)
+    def _():
+        kx_out[...] = k_sum.result(()).astype(BF16)
+        kx_copy().start()
+        s_gate_out[...], s_cot[z, x] = cotangents(ks_sum.result(()), s_pre)
+        for way in (0, 1):
+            gate_next(way)[0].start()
+        gate_copies()[0].start()
+        l_all.begin_split()
+        kx_copy().wait_recv()
+        gate_out[...], cot[z] = cotangents(kx_out[...].astype(F32) + kx_into[...].astype(F32), pre)
+        for way in (0, 1):
+            gate_next(way)[1].start()
+        l_all.begin_whole()
+        gate_copies()[1].start()
+
+    j_all.step(1)
+
+    @pl.when(teacher)
+    def _():
+        gate_copies()[0].wait_recv()
+        l_all.x_copy(0, 0).start()
+
+    tokens.drain()
+    for apart in range(1, 8):
+        hand(apart).wait_send()
+        for b in halves:
+            d_copy(b, apart).wait_send()
+    b_sum.drain()
+    s_sum.drain()
+    for g in (0, 1):
+        bx_copy(g).wait_send()
+    l_all.step(1)
     loss.over_x()
-
-    def kx_copy(h):
-        return remote(kx_out.at[h], kx_into.at[h], bx_s.at[2, h], bx_r.at[2, h], place.x_other)
-
-    def gate_copy(h):
-        return remote(gate_out.at[h], cot.at[z, h], g_s.at[h], g_r.at[h], place.partner)
-
-    l_all = HalfGather(place, cot, l_s, l_r)
-
-    def gate_next(way, h):
-        return remote(
-            gate_out.at[h], cot.at[z, h], gn_s.at[way, h], l_r.at[way, 0, h], place.z_next_cross[way]
-        )
-
-    @pl.when(student)
-    def _():
-        for h in halves:
-            kx_out[h] = k_sum.result((h,)).astype(BF16)
-            kx_copy(h).start()
-        factor = (16.0 * MODEL) / stat[0:1, 0:1]
-        for h in halves:
-            kx_copy(h).wait_recv()
-            hidden_cot = (kx_out[h].astype(F32) + kx_into[h].astype(F32)) * factor
-            gate_pre, up_pre = pre[h, 0], pre[h, 1]
-            sig = jax.nn.sigmoid(gate_pre)
-            gate_out[h] = (hidden_cot * up_pre * sig * (1.0 + gate_pre * (1.0 - sig))).astype(BF16)
-            for way in (0, 1):
-                gate_next(way, h).start()
-            cot[z, h] = (hidden_cot * gate_pre * sig).astype(BF16)
-            l_all.begin(h)
-            gate_copy(h).start()
-
-    j_all.step(1)
+    j_all.step(2)
+    c_all.drain()
+    e_sum.drain()
     loss.over_z()
-    l_all.step(1)
-    j_all.step(2)
-    loss.over_role()
     l_all.step(2)
     j_all.step(3)
+    loss.over_role()
+    d_partner().wait_send()
+    for apart in range(1, 8):
+        err_copy(apart).wait_send()
+    ex_copy().wait_send()
+    norm.drain()
     stat[...] = stat[...] + loss.result()
     stores.append(pltpu.make_async_copy(stat, stat_out, store_sem.at[4]))
     stores[-1].start()
@@ -598,30 +751,15 @@
 
     @pl.when(teacher)
     def _():
-        for h in halves:
-            gate_copy(h).wait_recv()
-
-    for h in halves:
-        l_all.last(h)
-        stores.append(
-            pltpu.make_async_copy(cot.at[:, h], cot_out.at[:, :, h * HALF : (h + 1) * HALF], store_sem.at[7 + h])
-        )
+        gate_copies()[1].wait_recv()
+
+    l_all.last_split()
+    l_all.last_whole()
+    l_all.wait_pair()
+    for i, (here, there) in enumerate(parts_of(cot, s_cot, cot_out)):
+        stores.append(pltpu.make_async_copy(here, there, store_sem.at[10 + i]))
         stores[-1].start()
 
-    tokens.drain()
-    for apart in range(1, 8):
-        hand(apart).wait_send()
-        err_copy(apart).wait_send()
-        for b in halves:
-            d_copy(b, apart).wait_send()
-    d_partner().wait_send()
-    b_sum.drain()
-    for h, g in tags:
-        bx_copy(h, g).wait_send()
-    c_all.drain()
-    e_sum.drain()
-    ex_copy().wait_send()
-    norm.drain()
     loss.drain()
     j_all.drain()
     for b in halves:
@@ -634,24 +772,23 @@
     @pl.when(student)
     def _():
         k_sum.drain()
+        ks_sum.drain()
         l_all.drain()
         err_share().wait_send()
         err_store().wait()
-        for h in halves:
-            kx_copy(h).wait_send()
-            gate_copy(h).wait_send()
-            for way in (0, 1):
-                gate_next(way, h).wait_send()
-            hid_share(h).wait_send()
-            hid_store(h).wait()
+        kx_copy().wait_send()
+        for copy in gate_copies() + gate_next(0) + gate_next(1) + hid_shares():
+            copy.wait_send()
+        for copy in hid_stores():
+            copy.wait()
 
     @pl.when(teacher)
     def _():
         l_all.drain(2)
         err_partner().wait_send()
         err_share().wait_recv()
-        for h in halves:
-            hid_share(h).wait_recv()
+        for copy in hid_shares():
+            copy.wait_recv()
 
     for b in halves:
         lin_arrival(b).wait_recv()
@@ -687,24 +824,30 @@
         out_specs=[anywhere] * 6,
         scratch_shapes=[
             vmem(2, Z, ROWS, QUARTER), vmem(WIDTH, 2 * UNITS), vmem(UNITS, WIDTH), vmem(2, WIDTH, QUARTER),
-            vmem(2, 2, Z, ROWS, HALF, dtype=F32), vmem(2, 4, 2, 2, ROWS, HALF), vmem(2, 4, 2, 2, ROWS, HALF),
-            vmem(2, 2, ROWS, HALF), vmem(2, 2, ROWS, HALF), vmem(2, 2, ROWS, HALF, dtype=F32), vmem(Z, 2, ROWS, HALF),
+            vmem(2, Z, ROWS, WHOLE, dtype=F32), vmem(2, 4, 2, ROWS, WHOLE), vmem(2, 4, 2, ROWS, WHOLE),
+            vmem(2, ROWS, WHOLE), vmem(2, ROWS, WHOLE), vmem(2, ROWS, WHOLE, dtype=F32), vmem(Z, ROWS, WHOLE),
+            vmem(2, 2, Z, ROWS, SPLIT, dtype=F32), vmem(2, 4, 2, ROWS, SPLIT), vmem(2, 4, 2, ROWS, SPLIT),
+            vmem(Z, 2, ROWS, SPLIT), vmem(Z, 2, ROWS, SPLIT), vmem(2, ROWS, SPLIT, dtype=F32), vmem(Z, 2, ROWS, SPLIT),
             vmem(Z * ROWS, WIDTH, dtype=F32), vmem(2, 8, ROWS, QUARTER), vmem(2, 8, ROWS, QUARTER),
             vmem(2, 8, ROWS, QUARTER), vmem(ROWS, QUARTER), vmem(ROWS, QUARTER),
             vmem(2, Z, ROWS, QUARTER, dtype=F32), vmem(2, 4, 2, ROWS, QUARTER), vmem(2, 4, 2, ROWS, QUARTER),
             vmem(ROWS, QUARTER), vmem(ROWS, QUARTER), vmem(Z, 2, ROWS, QUARTER),
-            vmem(2, 4, 2, ROWS, HALF), vmem(2, 4, 2, ROWS, HALF), vmem(2, ROWS, HALF), vmem(2, ROWS, HALF),
-            vmem(2, ROWS, HALF), vmem(Z, 2, ROWS, HALF),
+            vmem(2, 4, ROWS, WHOLE), vmem(2, 4, ROWS, WHOLE), vmem(ROWS, WHOLE), vmem(ROWS, WHOLE),
+            vmem(ROWS, WHOLE), vmem(Z, ROWS, WHOLE),
+            vmem(2, 4, ROWS, SPLIT), vmem(2, 4, ROWS, SPLIT), vmem(Z, ROWS, SPLIT), vmem(Z, ROWS, SPLIT),
+            vmem(ROWS, SPLIT), vmem(Z, 2, ROWS, SPLIT),
             *total_tiles(), *total_tiles(), vmem(8, 128, dtype=F32),
-            sems(6), sems(9),
-            sems(7), sems(7), sems(7), sems(7), sems(2, 4, 2, 2), sems(2, 4, 2, 2), sems(3, 2), sems(3, 2),
-            sems(2, 4, 2), sems(2, 4, 2),
+            sems(6), sems(13),
+            sems(7), sems(7), sems(7), sems(7), sems(2, 4, 2), sems(2, 4, 2), sems(3), sems(3),
+            sems(2, 4, 2), sems(2, 4, 2), sems(8), sems(8),
+            sems(2, 4), sems(2, 4), sems(2, 4), sems(2, 4), sems(8), sems(8),
             sems(2, 7), sems(2, 7), sems(4), sems(4), sems(7), sems(2, 7), sems(2, 4, 2), sems(2, 4, 2),
-            sems(2, 4, 2), sems(2, 4, 2),
-            sems(2, 4, 2), sems(2, 4, 2), sems(1), sems(1), sems(2, 4, 2), sems(2, 4, 2), sems(2), sems(2), sems(2, 2),
+            sems(2, 4), sems(2, 4), sems(2, 4), sems(2, 4), sems(8), sems(8),
+            sems(2, 4, 2), sems(2, 4, 2), sems(1), sems(1),
+            sems(2, 4), sems(2, 4), sems(2, 4), sems(2, 4), sems(8), sems(8), sems(2), sems(2), sems(2, 2),
             sems(7), sems(7), sems(7), sems(7), sems(2), sems(2),
             sems(7), sems(7), sems(7), sems(7), sems(2), sems(2),
-            sems(5), sems(5),
+            sems(8), sems(8),
         ],
         compiler_params=pltpu.CompilerParams(
             collective_id=0, has_side_effects=True, vmem_limit_bytes=34 * 1024 * 1024

time: 133 us -> 134 us (level); the launches traced: 133 us -> 133 us
  no operation moved by 1% of the time
where the time goes in v3:
time: 134 us; the launch traced here: 133 us
  Pallas kernels  129 us (96%)
  local copies, waits for them, and re-layouts  2.84 us (2%)
    pallas_call x1, Pallas kernels, exchange(): pl.pallas_call(exchange_kernel, out_shape=[array(2, Z, ROWS, QUARTER), ar...  123 us
    pallas_call x1, Pallas kernels, gradients(): pl.pallas_call(gradients_kernel, grid=(UNITS // BLOCK,), out_shape=[jax.S...  6.27 us
    unnamed x7, local copies, waits for them, and re-layouts  2.84 us

profile of v3, /device:TPU:1, one launch (start us, length us, event | category | flops | bytes accessed | tf_op | source)
XLA Modules:
  0.0 132.5 jit_solution(11757045867117021068)
XLA Ops:
  0.6 0.0 copy-start
  0.6 0.0 copy-start.1
  0.7 0.0 copy-start.2
  0.7 2.8 %copy.8 = bf16[64,8,2,1792]{3,1,2,0:T(8,128)(2,1)S(1)} copy(bf16[64,8,2,1792]{3,2,1,0:T(2,128)(2,1)} %bitcast.17) | data formatting | bytes 7340032
  3.4 0.0 copy-done
  3.5 0.1 copy-done.1
  3.5 0.0 copy-done.2
  3.5 122.8 %exchange.1 = (bf16[2,8,48,256]{3,2,1,0:T(8,128)(2,1)S(1)}, bf16[8,48,1792]{2,1,0:T(8,128)(2,1)S(1)}, bf16[8,48,1792]{2,1,0:T(8,128)(2,1)S(1)}, bf16[2,8,48,256]...) custom-call(bf16[48,512]{1,0:T(8,128)(2,1)S(1)} %copy-done.2, ...), custom_call_target="tpu_custom_call" | custom-call | tf_op jit(solution)/shard_map/exchange/pallas_call | solution.py:813
  126.3 6.3 %gradients.1 = (bf16[512,1792]{1,0:T(8,128)(2,1)}, bf16[1792,512]{1,0:T(8,128)(2,1)}, bf16[512,1024]{1,0:T(8,128)(2,1)}, f32[2]{0:T(128)}) custom-call(bf16[2,384,256]{2,1,0:T(8,128)(2,1)S(1)} %bitcast.15, bf16[384,1792]{1,0:T(8,128)(2,1)S(1)} %bitcast.12, bf16[384,1792]{1,0:T(8,128)(2,1)S(1)} %bitcast.13, bf16[2,384,256]{2,1,0:T(8,128)(2,1)S(1)} %bitcast.16, ...), custom_call_target="tpu_custom_call" | custom-call | tf_op jit(solution)/shard_map/gradients/pallas_call | solution.py:891
Async XLA Ops:
  0.6 2.8 %copy-start = (bf16[1,1792,512]{2,1,0:T(8,128)(2,1)S(1)}, bf16[1,1792,512]{2,1,0:T(8,128)(2,1)}, u32[]{:S(2)}) copy-start(bf16[1,1792,512]{2,1,0:T(8,128)(2,1)} %param.6) | copy-start | bytes 5505028
  0.6 2.9 %copy-start.1 = (bf16[512,1024]{1,0:T(8,128)(2,1)S(1)}, bf16[512,1024]{1,0:T(8,128)(2,1)}, u32[]{:S(2)}) copy-start(bf16[512,1024]{1,0:T(8,128)(2,1)} %lin_in.1) | copy-start | bytes 3145732
  0.7 2.9 %copy-start.2 = (bf16[48,512]{1,0:T(8,128)(2,1)S(1)}, bf16[48,512]{1,0:T(8,128)(2,1)}, u32[]{:S(2)}) copy-start(bf16[48,512]{1,0:T(8,128)(2,1)} %tok_in.1) | copy-start | bytes 147460

commit v4 on v3

--- a/solution.py
+++ b/solution.py
@@ -12,8 +12,8 @@
 ROWS = 48
 WIDTH = 512
 UNITS = 1792
-WHOLE = 1024
-SPLIT = 384
+WHOLE = 768
+SPLIT = 512
 LIN = 1024
 QUARTER = LIN // 4
 
@@ -134,8 +134,8 @@
             self.x_out.at[block], self.x_into.at[block], self.x_send.at[offset], self.x_recv.at[offset], self.place.x_other
         )
 
-    def exchange(self):
-        for offset in (4, 3, 5, 2, 6, 1, 7, 0):
+    def exchange(self, offsets):
+        for offset in offsets:
             block = self.block(offset)
             for tag in self.tags:
                 self.x_out[(block,) + tag] = self.other[tag + (block,)].astype(BF16)
@@ -420,24 +420,25 @@
             ).reshape(Z, ROWS, SPLIT)
 
     split_dot(0)
-    s_sum.exchange()
+    s_sum.exchange((4, 3, 5))
     for g in (0, 1):
         part[g] = jnp.dot(
             all_tokens(), w[:, g * UNITS : g * UNITS + WHOLE], preferred_element_type=F32
         ).reshape(Z, ROWS, WHOLE)
         b_sum.begin((g,))
     split_dot(1)
+    b_sum.step(2)
+    s_sum.exchange((2, 6, 1, 7, 0))
     for tag in tags:
         s_sum.begin(tag)
-    b_sum.step(2)
-    s_sum.step(2)
     for load in loads[3:]:
         load.wait()
     for q in (0, 1):
         lin_part[q] = jnp.dot(all_tokens(), lin[x_of[q]], preferred_element_type=F32).reshape(Z, ROWS, QUARTER)
-    for step in (3, 4):
-        b_sum.step(step)
-        s_sum.step(step)
+    b_sum.step(3)
+    s_sum.step(2)
+    b_sum.step(4)
+    s_sum.step(3)
 
     def bx_copy(g):
         return remote(bx_out.at[g], bx_into.at[g], bx_s.at[g], bx_r.at[g], place.x_other)
@@ -445,6 +446,7 @@
     for g in (0, 1):
         bx_out[g] = b_sum.result((g,)).astype(BF16)
         bx_copy(g).start()
+    s_sum.step(4)
 
     def hidden(inputs):
         return (inputs[0] * jax.nn.sigmoid(inputs[0]) * inputs[1]).astype(BF16)
@@ -602,11 +604,10 @@
                 err_arrival(source_role, apart).wait_recv()
         err_partner().wait_recv()
         s_part[0, 0] = cot_dot(pl.multiple_of(WHOLE + x_of[0] * SPLIT, 128), SPLIT)
-        ks_sum.exchange()
+        ks_sum.exchange((4, 3, 5, 2, 6, 1, 7, 0))
         part[0] = cot_dot(0, WHOLE)
         k_sum.begin(())
         s_part[1, 0] = cot_dot(pl.multiple_of(WHOLE + x_of[1] * SPLIT, 128), SPLIT)
-        ks_sum.begin(())
         err_share().start()
         err_store().start()
         for copy in hid_shares() + hid_stores():
@@ -619,7 +620,7 @@
     @pl.when(student)
     def _():
         k_sum.step(2)
-        ks_sum.step(2)
+        ks_sum.begin(())
 
     def ex_copy():
         return remote(ex_out, ex_into, one_s.at[3], one_r.at[3], place.x_other)
@@ -632,7 +633,7 @@
     @pl.when(student)
     def _():
         k_sum.step(3)
-        ks_sum.step(3)
+        ks_sum.step(2)
 
     ex_copy().wait_recv()
 
@@ -650,27 +651,23 @@
     @pl.when(student)
     def _():
         k_sum.step(4)
-        ks_sum.step(4)
+        ks_sum.step(3)
 
     stat[...] = norm.result()
     j_all.begin_other()
+    loss.over_x()
 
     def kx_copy():
         return remote(kx_out, kx_into, bx_s.at[2], bx_r.at[2], place.x_other)
 
-    def gate_copies():
-        return [
-            remote(s_gate_out, s_cot.at[z, x], g_s.at[0], g_r.at[0], place.partner),
-            remote(gate_out, cot.at[z], g_s.at[1], g_r.at[1], place.partner),
-        ]
+    def gate_copy(i):
+        return remote(*((s_gate_out, s_cot.at[z, x]), (gate_out, cot.at[z]))[i], g_s.at[i], g_r.at[i], place.partner)
 
     l_all = Gather(place, cot, s_cot, l_s, l_r, ls_s, ls_r, lx_s, lx_r)
 
-    def gate_next(way):
-        return [
-            remote(s_gate_out, s_cot.at[z, x], gn_s.at[way, 0], ls_r.at[way, 0], place.z_next_cross[way]),
-            remote(gate_out, cot.at[z], gn_s.at[way, 1], l_r.at[way, 0], place.z_next_cross[way]),
-        ]
+    def gate_next(way, i):
+        ends = ((s_gate_out, s_cot.at[z, x]), (gate_out, cot.at[z]))[i]
+        return remote(*ends, gn_s.at[way, i], (ls_r, l_r)[i].at[way, 0], place.z_next_cross[way])
 
     def cotangents(total, inputs):
         factor = (16.0 * MODEL) / stat[0:1, 0:1]
@@ -684,23 +681,24 @@
     def _():
         kx_out[...] = k_sum.result(()).astype(BF16)
         kx_copy().start()
+        ks_sum.step(4)
         s_gate_out[...], s_cot[z, x] = cotangents(ks_sum.result(()), s_pre)
         for way in (0, 1):
-            gate_next(way)[0].start()
-        gate_copies()[0].start()
+            gate_next(way, 0).start()
+        gate_copy(0).start()
         l_all.begin_split()
         kx_copy().wait_recv()
         gate_out[...], cot[z] = cotangents(kx_out[...].astype(F32) + kx_into[...].astype(F32), pre)
         for way in (0, 1):
-            gate_next(way)[1].start()
+            gate_next(way, 1).start()
         l_all.begin_whole()
-        gate_copies()[1].start()
+        gate_copy(1).start()
 
     j_all.step(1)
 
     @pl.when(teacher)
     def _():
-        gate_copies()[0].wait_recv()
+        gate_copy(0).wait_recv()
         l_all.x_copy(0, 0).start()
 
     tokens.drain()
@@ -712,12 +710,11 @@
     s_sum.drain()
     for g in (0, 1):
         bx_copy(g).wait_send()
+    loss.over_z()
     l_all.step(1)
-    loss.over_x()
     j_all.step(2)
     c_all.drain()
     e_sum.drain()
-    loss.over_z()
     l_all.step(2)
     j_all.step(3)
     loss.over_role()
@@ -726,10 +723,10 @@
         err_copy(apart).wait_send()
     ex_copy().wait_send()
     norm.drain()
+    l_all.step(3)
     stat[...] = stat[...] + loss.result()
     stores.append(pltpu.make_async_copy(stat, stat_out, store_sem.at[4]))
     stores[-1].start()
-    l_all.step(3)
     j_all.last()
 
     def lin_columns(b):
@@ -751,7 +748,7 @@
 
     @pl.when(teacher)
     def _():
-        gate_copies()[1].wait_recv()
+        gate_copy(1).wait_recv()
 
     l_all.last_split()
     l_all.last_whole()
@@ -777,7 +774,11 @@
         err_share().wait_send()
         err_store().wait()
         kx_copy().wait_send()
-        for copy in gate_copies() + gate_next(0) + gate_next(1) + hid_shares():
+        for i in (0, 1):
+            gate_copy(i).wait_send()
+            for way in (0, 1):
+                gate_next(way, i).wait_send()
+        for copy in hid_shares():
             copy.wait_send()
         for copy in hid_stores():
             copy.wait()
@@ -863,56 +864,47 @@
 BLOCK = 256
 
 
-def gradients_kernel(tok, cot, hid, err, lin_err, stat, unit_grad, down_grad, linear_grad, losses, turned):
-    step = pl.program_id(0)
+def gradients_kernel(tok, cot, hid, err, lin_err, stat, unit_out, down_out, linear_out, losses, turned, unit, down, linear, sem):
     factor = (16.0 * MODEL) / stat[0:1, 0:1]
-
-    @pl.when(step == 0)
-    def _():
+    share = stat[...] / stat[0:1, 0:1]
+    losses[0] = share[1, 0]
+    losses[1] = share[2, 0]
+    for b in (0, 1):
+        turned[b * QUARTER : (b + 1) * QUARTER] = tok[b].T
+    copies = []
+
+    def send(here, there):
+        copies.append(pltpu.make_async_copy(here, there, sem.at[len(copies)]))
+        copies[-1].start()
+
+    for i in range(UNITS // BLOCK):
+        part = slice(i * BLOCK, (i + 1) * BLOCK)
+        unit[:, part] = jnp.dot(turned[...], cot[:, part], preferred_element_type=F32).astype(BF16)
+        send(unit.at[:, part], unit_out.at[:, part])
         for b in (0, 1):
-            turned[b * QUARTER : (b + 1) * QUARTER] = tok[b].T
-        share = stat[...] / stat[0:1, 0:1]
-        losses[0] = share[1, 0]
-        losses[1] = share[2, 0]
-
-    unit_grad[...] = jnp.dot(turned[...], cot[...], preferred_element_type=F32).astype(BF16)
-    for b in (0, 1):
-        down_grad[:, b * QUARTER : (b + 1) * QUARTER] = (factor * contract_rows(hid[...], err[b])).astype(BF16)
-
-    @pl.when(step < LIN // BLOCK)
-    def _():
-        linear_grad[...] = (factor * jnp.dot(turned[...], lin_err[...], preferred_element_type=F32)).astype(BF16)
+            down[part, b * QUARTER : (b + 1) * QUARTER] = (factor * contract_rows(hid[:, part], err[b])).astype(BF16)
+        send(down.at[part], down_out.at[part])
+        if i < LIN // BLOCK:
+            product = jnp.dot(turned[...], lin_err[:, part], preferred_element_type=F32)
+            linear[:, part] = (factor * product).astype(BF16)
+            send(linear.at[:, part], linear_out.at[:, part])
+    for copy in copies:
+        copy.wait()
 
 
 def gradients(tok, cot, hid, err, lin_err, stat):
-    tokens = Z * ROWS
-    last = LIN // BLOCK - 1
-    halves = pl.BlockSpec((2, tokens, QUARTER), lambda i: (0, 0, 0))
+    shapes = [(WIDTH, UNITS), (UNITS, WIDTH), (WIDTH, LIN)]
     return pl.pallas_call(
         gradients_kernel,
-        grid=(UNITS // BLOCK,),
-        out_shape=[
-            jax.ShapeDtypeStruct((WIDTH, UNITS), BF16),
-            jax.ShapeDtypeStruct((UNITS, WIDTH), BF16),
-            jax.ShapeDtypeStruct((WIDTH, LIN), BF16),
-            jax.ShapeDtypeStruct((2,), F32),
+        out_shape=[jax.ShapeDtypeStruct(shape, BF16) for shape in shapes] + [jax.ShapeDtypeStruct((2,), F32)],
+        in_specs=[pl.BlockSpec(memory_space=pltpu.VMEM)] * 6,
+        out_specs=[pl.BlockSpec(memory_space=pl.ANY)] * 3 + [pl.BlockSpec(memory_space=pltpu.SMEM)],
+        scratch_shapes=[
+            pltpu.VMEM((WIDTH, Z * ROWS), BF16),
+            *[pltpu.VMEM(shape, BF16) for shape in shapes],
+            pltpu.SemaphoreType.DMA((2 * (UNITS // BLOCK) + LIN // BLOCK,)),
         ],
-        in_specs=[
-            halves,
-            pl.BlockSpec((tokens, BLOCK), lambda i: (0, i)),
-            pl.BlockSpec((tokens, BLOCK), lambda i: (0, i)),
-            halves,
-            pl.BlockSpec((tokens, BLOCK), lambda i: (0, jnp.minimum(i, last))),
-            pl.BlockSpec((8, 128), lambda i: (0, 0)),
-        ],
-        out_specs=[
-            pl.BlockSpec((WIDTH, BLOCK), lambda i: (0, i)),
-            pl.BlockSpec((BLOCK, WIDTH), lambda i: (i, 0)),
-            pl.BlockSpec((WIDTH, BLOCK), lambda i: (0, jnp.minimum(i, last))),
-            pl.BlockSpec(memory_space=pltpu.SMEM),
-        ],
-        scratch_shapes=[pltpu.VMEM((WIDTH, tokens), BF16)],
-        compiler_params=pltpu.CompilerParams(vmem_limit_bytes=16 * 1024 * 1024),
+        compiler_params=pltpu.CompilerParams(vmem_limit_bytes=24 * 1024 * 1024),
         name="gradients",
     )(tok, cot, hid, err, lin_err, stat)
 

time: 134 us -> 126 us (0.940); the launches traced: 133 us -> 126 us
  Pallas kernels: 129 us -> 123 us
    pallas_call x1, Pallas kernels: 123 us -> 119 us  [exchange(): pl.pallas_call(exchange_kernel, out_shape=[array(2, Z, ROWS, QUARTER), ar...]
    pallas_call x1, Pallas kernels: 6.27 us -> 4.11 us  [gradients(): pl.pallas_call(gradients_kernel, out_shape=[jax.ShapeDtypeStruct(shape, B...]
where the time goes in v4:
time: 126 us
  Pallas kernels  123 us (98%)
  local copies, waits for them, and re-layouts  2.84 us (2%)
    pallas_call x1, Pallas kernels, exchange(): pl.pallas_call(exchange_kernel, out_shape=[array(2, Z, ROWS, QUARTER), ar...  119 us
    pallas_call x1, Pallas kernels, gradients(): pl.pallas_call(gradients_kernel, out_shape=[jax.ShapeDtypeStruct(shape, B...  4.11 us
    unnamed x7, local copies, waits for them, and re-layouts  2.84 us

profile of v4, /device:TPU:1, one launch (start us, length us, event | category | flops | bytes accessed | tf_op | source)
XLA Modules:
  0.0 126.4 jit_solution(4066629432855263890)
XLA Ops:
  0.6 0.0 copy-start
  0.6 0.0 copy-start.1
  0.7 0.0 copy-start.2
  0.7 2.8 %copy.8 = bf16[64,8,2,1792]{3,1,2,0:T(8,128)(2,1)S(1)} copy(bf16[64,8,2,1792]{3,2,1,0:T(2,128)(2,1)} %bitcast.17) | data formatting | bytes 7340032
  3.4 0.0 copy-done
  3.5 0.1 copy-done.1
  3.5 0.0 copy-done.2
  3.5 118.8 %exchange.1 = (bf16[2,8,48,256]{3,2,1,0:T(8,128)(2,1)S(1)}, bf16[8,48,1792]{2,1,0:T(8,128)(2,1)S(1)}, bf16[8,48,1792]{2,1,0:T(8,128)(2,1)S(1)}, bf16[2,8,48,256]...) custom-call(bf16[48,512]{1,0:T(8,128)(2,1)S(1)} %copy-done.2, ...), custom_call_target="tpu_custom_call" | custom-call | tf_op jit(solution)/shard_map/exchange/pallas_call | solution.py:814
  122.3 4.1 %gradients.1 = (bf16[512,1792]{1,0:T(8,128)(2,1)}, bf16[1792,512]{1,0:T(8,128)(2,1)}, bf16[512,1024]{1,0:T(8,128)(2,1)}, f32[2]{0:T(128)}) custom-call(bf16[2,384,256]{2,1,0:T(8,128)(2,1)S(1)} %bitcast.15, bf16[384,1792]{1,0:T(8,128)(2,1)S(1)} %bitcast.12, bf16[384,1792]{1,0:T(8,128)(2,1)S(1)} %bitcast.13, bf16[2,384,256]{2,1,0:T(8,128)(2,1)S(1)} %bitcast.16, ...), custom_call_target="tpu_custom_call" | custom-call | tf_op jit(solution)/shard_map/gradients/pallas_call | solution.py:897
Async XLA Ops:
  0.6 2.8 %copy-start = (bf16[1,1792,512]{2,1,0:T(8,128)(2,1)S(1)}, bf16[1,1792,512]{2,1,0:T(8,128)(2,1)}, u32[]{:S(2)}) copy-start(bf16[1,1792,512]{2,1,0:T(8,128)(2,1)} %param.6) | copy-start | bytes 5505028
  0.6 2.9 %copy-start.1 = (bf16[512,1024]{1,0:T(8,128)(2,1)S(1)}, bf16[512,1024]{1,0:T(8,128)(2,1)}, u32[]{:S(2)}) copy-start(bf16[512,1024]{1,0:T(8,128)(2,1)} %lin_in.1) | copy-start | bytes 3145732
  0.7 2.9 %copy-start.2 = (bf16[48,512]{1,0:T(8,128)(2,1)S(1)}, bf16[48,512]{1,0:T(8,128)(2,1)}, u32[]{:S(2)}) copy-start(bf16[48,512]{1,0:T(8,128)(2,1)} %tok_in.1) | copy-start | bytes 147460

commit v5 on v4

--- a/solution.py
+++ b/solution.py
@@ -47,16 +47,19 @@
     def local(self, tag, offset):
         return self.part[tag + (lax.rem(self.place.z + offset + Z, Z),)]
 
-    def begin(self, tag):
+    def begin(self, tag, both=True):
         far = self.long_way(tag)
         self.push(far, 1, tag, True)
-        self.push(1 - far, 2, tag, True)
-
-    def step(self, step, tags=None):
-        for tag in tags or self.tags:
+        if both:
+            self.push(1 - far, 2, tag, True)
+
+    def step(self, step, both=False):
+        for tag in self.tags:
             for way in (0, 1):
                 if step > 2 or way == self.long_way(tag):
                     self.push(way, step, tag, False)
+                elif both:
+                    self.push(way, step, tag, True)
 
     def result(self, tag):
         total = self.local(tag, 0)
@@ -164,31 +167,33 @@
     def block(self, way, steps):
         return lax.rem(self.place.z - (1 - 2 * way) * steps + Z, Z)
 
-    def w_copy(self, way, step, arriving=False):
+    def w_copy(self, way, step, arriving=False, source=None):
         part = self.whole.at[self.block(way, step if arriving else step - 1)]
         if step == 4:
             part = part.at[:, way * WHOLE // 2 : (way + 1) * WHOLE // 2]
         at = (way, step - 1)
-        return remote(part, part, self.w_send.at[at], self.w_recv.at[at], self.place.z_next[way])
-
-    def s_copy(self, way, step, arriving=False):
+        return remote(part if source is None else source, part, self.w_send.at[at], self.w_recv.at[at], self.place.z_next[way])
+
+    def s_copy(self, way, step, arriving=False, source=None):
         part = self.split.at[self.block(way, step if arriving else step - 1), self.place.x]
         at = (way, step - 1)
-        return remote(part, part, self.s_send.at[at], self.s_recv.at[at], self.place.z_next[way])
-
-    def x_copy(self, way, steps, arriving=False):
+        return remote(part if source is None else source, part, self.s_send.at[at], self.s_recv.at[at], self.place.z_next[way])
+
+    def x_copy(self, way, steps, arriving=False, source=None):
         part = self.split.at[self.block(way, steps), 1 - self.place.x if arriving else self.place.x]
         at = steps + 3 * way if steps else 0
-        return remote(part, part, self.x_send.at[at], self.x_recv.at[at], self.place.x_other)
-
-    def begin_split(self):
+        return remote(
+            part if source is None else source, part, self.x_send.at[at], self.x_recv.at[at], self.place.x_other
+        )
+
+    def begin_split(self, source=None):
         for way in (0, 1):
-            self.s_copy(way, 1).start()
-        self.x_copy(0, 0).start()
-
-    def begin_whole(self):
+            self.s_copy(way, 1, source=source).start()
+        self.x_copy(0, 0, source=source).start()
+
+    def begin_whole(self, source=None):
         for way in (0, 1):
-            self.w_copy(way, 1).start()
+            self.w_copy(way, 1, source=source).start()
 
     def step(self, step):
         for way in (0, 1):
@@ -320,21 +325,21 @@
 
 def exchange_kernel(
     tok_in, w_in, down_in, lin_in,
-    tok_out, cot_out, hid_out, err_out, lin_out, stat_out,
-    tok, w, down, lin,
+    tok_out, cot, s_cot, hid_out, err_out, lin_out, stat_out,
+    tok, w, down, lin, down_turned,
     part, b_out, b_into, bx_out, bx_into, pre, hid,
     s_part, s_out, s_into, sx_out, sx_into, s_pre, s_hid,
     d_part, d_out, d_into, err, target_out, target,
     lin_part, e_out, e_into, ex_out, ex_into, lin_err,
-    k_out, k_into, kx_out, kx_into, gate_out, cot,
-    ks_out, ks_into, ksx_out, ksx_into, s_gate_out, s_cot,
-    m1, z1, x1, x1_got, r1, r1_got, m2, z2, x2, x2_got, r2, r2_got, stat,
+    k_out, k_into, kx_out, kx_into, gate_out, up_out,
+    ks_out, ks_into, ksx_out, ksx_into, s_gate_out, s_up_out,
+    m1, z1, x1, x1_got, r1, r1_got, stat,
     load_sem, store_sem,
     tok_s, tok_r, hand_s, hand_r, b_s, b_r, bx_s, bx_r, s_s, s_r, sx_s, sx_r,
     c_s, c_r, cs_s, cs_r, cx_s, cx_r,
     d_s, d_r, one_s, one_r, i_s, i_r, e_s, e_r, k_s, k_r, ks_s, ks_r, ksx_s, ksx_r,
     j_s, j_r, jx_s, jx_r, l_s, l_r, ls_s, ls_r, lx_s, lx_r, g_s, g_r, gn_s,
-    m1_s, m1_r, z1_s, z1_r, o1_s, o1_r, m2_s, m2_r, z2_s, z2_r, o2_s, o2_r,
+    m1_s, m1_r, z1_s, z1_r, o1_s, o1_r,
     share_s, share_r,
 ):
     place = Place()
@@ -420,25 +425,31 @@
             ).reshape(Z, ROWS, SPLIT)
 
     split_dot(0)
-    s_sum.exchange((4, 3, 5))
+    s_sum.exchange((4,))
     for g in (0, 1):
         part[g] = jnp.dot(
             all_tokens(), w[:, g * UNITS : g * UNITS + WHOLE], preferred_element_type=F32
         ).reshape(Z, ROWS, WHOLE)
         b_sum.begin((g,))
+        if g == 0:
+            s_sum.exchange((3, 5))
     split_dot(1)
+    for tag in tags:
+        s_sum.begin(tag, False)
     b_sum.step(2)
-    s_sum.exchange((2, 6, 1, 7, 0))
-    for tag in tags:
-        s_sum.begin(tag)
+    s_sum.exchange((2, 6))
     for load in loads[3:]:
         load.wait()
     for q in (0, 1):
         lin_part[q] = jnp.dot(all_tokens(), lin[x_of[q]], preferred_element_type=F32).reshape(Z, ROWS, QUARTER)
+    s_sum.step(2, True)
     b_sum.step(3)
-    s_sum.step(2)
+    s_sum.exchange((1, 7, 0))
+    for c in range(UNITS // QUARTER):
+        down_turned[:, c * QUARTER : (c + 1) * QUARTER] = down[c * QUARTER : (c + 1) * QUARTER].T
+    s_sum.step(3)
     b_sum.step(4)
-    s_sum.step(3)
+    s_sum.step(4)
 
     def bx_copy(g):
         return remote(bx_out.at[g], bx_into.at[g], bx_s.at[g], bx_r.at[g], place.x_other)
@@ -446,7 +457,6 @@
     for g in (0, 1):
         bx_out[g] = b_sum.result((g,)).astype(BF16)
         bx_copy(g).start()
-    s_sum.step(4)
 
     def hidden(inputs):
         return (inputs[0] * jax.nn.sigmoid(inputs[0]) * inputs[1]).astype(BF16)
@@ -462,10 +472,11 @@
     hid[z] = hidden(pre)
     c_all.begin_whole()
     e_sum = RingSum(place, lin_part, e_out, e_into, e_s, e_r, [(0,), (1,)], lambda tag: tag[0])
+    for tag in e_sum.tags:
+        e_sum.begin(tag)
     for step in (1, 2, 3):
         c_all.step(step)
-    for tag in e_sum.tags:
-        e_sum.begin(tag)
+        e_sum.step(step + 1)
 
     c_all.last_split()
     c_all.last_whole()
@@ -504,7 +515,20 @@
             d_copy(b, apart).start()
     d_partner().start()
     d_into[role, mp] = d_out[role, mp]
-    e_sum.step(2)
+
+    def ex_copy():
+        return remote(ex_out, ex_into, one_s.at[3], one_r.at[3], place.x_other)
+
+    ex_out[...] = e_sum.result((0,)).astype(BF16)
+    ex_copy().start()
+    linear_rows = e_sum.result((1,))
+    tokens.drain()
+    b_sum.drain()
+    s_sum.drain()
+    for apart in range(1, 8):
+        hand(apart).wait_send()
+    for g in (0, 1):
+        bx_copy(g).wait_send()
     for apart in (1, 7, 2, 6, 3, 5, 4):
         for source_role in (0, 1):
             d_arrival(source_role, apart).wait_recv()
@@ -554,14 +578,6 @@
     def _():
         target[...] = target_out[...]
 
-    row = lax.broadcasted_iota(jnp.int32, (8, 128), 0)
-    teacher_float = teacher_rows.astype(F32)
-    target_square = jnp.sum(teacher_float * teacher_float)
-    error_square = jnp.sum(error * error)
-    norm = Total(place, m1, z1, x1, x1_got, r1, r1_got, m1_s, m1_r, z1_s, z1_r, o1_s, o1_r)
-    norm.start(jnp.where(row == 0, target_square, jnp.where(row == 1, error_square, 0.0)))
-    e_sum.step(3)
-
     k_sum = RingSum(place, part.at[0], k_out, k_into, k_s, k_r, [()], lambda tag: 0)
     ks_sum = PairRingSum(place, s_part.at[1, 0], ks_out, ks_into, ks_s, ks_r, [()], lambda tag: 1)
     ks_sum.pair(s_part.at[0, 0], ksx_out, ksx_into, ksx_s, ksx_r)
@@ -590,12 +606,8 @@
         ]
 
     def cot_dot(start, size):
-        return lax.dot_general(
-            jnp.concatenate([err[b].reshape(Z * ROWS, QUARTER) for b in halves], axis=1),
-            down[pl.ds(start, size)],
-            (((1,), (1,)), ((), ())),
-            preferred_element_type=F32,
-        ).reshape(Z, ROWS, size)
+        all_err = jnp.concatenate([err[b].reshape(Z * ROWS, QUARTER) for b in halves], axis=1)
+        return jnp.dot(all_err, down_turned[:, pl.ds(start, size)], preferred_element_type=F32).reshape(Z, ROWS, size)
 
     @pl.when(student)
     def _():
@@ -604,37 +616,17 @@
                 err_arrival(source_role, apart).wait_recv()
         err_partner().wait_recv()
         s_part[0, 0] = cot_dot(pl.multiple_of(WHOLE + x_of[0] * SPLIT, 128), SPLIT)
-        ks_sum.exchange((4, 3, 5, 2, 6, 1, 7, 0))
+        ks_sum.exchange((4,))
         part[0] = cot_dot(0, WHOLE)
         k_sum.begin(())
+        ks_sum.exchange((3, 5))
         s_part[1, 0] = cot_dot(pl.multiple_of(WHOLE + x_of[1] * SPLIT, 128), SPLIT)
+        ks_sum.exchange((2, 6, 1, 7, 0))
         err_share().start()
         err_store().start()
         for copy in hid_shares() + hid_stores():
             copy.start()
 
-    norm.over_x()
-    e_sum.step(4)
-    norm.over_z()
-
-    @pl.when(student)
-    def _():
-        k_sum.step(2)
-        ks_sum.begin(())
-
-    def ex_copy():
-        return remote(ex_out, ex_into, one_s.at[3], one_r.at[3], place.x_other)
-
-    ex_out[...] = e_sum.result((0,)).astype(BF16)
-    ex_copy().start()
-    linear_rows = e_sum.result((1,))
-    norm.over_role()
-
-    @pl.when(student)
-    def _():
-        k_sum.step(3)
-        ks_sum.step(2)
-
     ex_copy().wait_recv()
 
     @pl.when(z != mp)
@@ -645,23 +637,51 @@
     lin_err[z, x] = linear_error.astype(BF16)
     j_all = RingGather(place, lin_err, j_s, j_r, jx_s.at[0], jx_r.at[0])
     j_all.begin()
-    loss = Total(place, m2, z2, x2, x2_got, r2, r2_got, m2_s, m2_r, z2_s, z2_r, o2_s, o2_r)
-    loss.start(jnp.where(row == 2, jnp.sum(linear_error * linear_error), 0.0))
+    row = lax.broadcasted_iota(jnp.int32, (8, 128), 0)
+    teacher_float = teacher_rows.astype(F32)
+    norm = Total(place, m1, z1, x1, x1_got, r1, r1_got, m1_s, m1_r, z1_s, z1_r, o1_s, o1_r)
+    target_square = jnp.sum(teacher_float * teacher_float)
+    error_square = jnp.sum(error * error)
+    linear_square = jnp.sum(linear_error * linear_error)
+    norm.start(jnp.where(row == 0, target_square, jnp.where(row == 1, error_square, linear_square)))
 
     @pl.when(student)
     def _():
+        ks_sum.begin((), False)
+        k_sum.step(2)
+
+    j_all.begin_other()
+    norm.over_x()
+
+    @pl.when(student)
+    def _():
+        ks_sum.step(2, True)
+        k_sum.step(3)
+
+    norm.over_z()
+    j_all.step(1)
+
+    @pl.when(student)
+    def _():
+        ks_sum.step(3)
         k_sum.step(4)
-        ks_sum.step(3)
-
+        ks_sum.step(4)
+
+    norm.over_role()
+    j_all.step(2)
     stat[...] = norm.result()
-    j_all.begin_other()
-    loss.over_x()
+    stores.append(pltpu.make_async_copy(stat, stat_out, store_sem.at[4]))
+    stores[-1].start()
 
     def kx_copy():
         return remote(kx_out, kx_into, bx_s.at[2], bx_r.at[2], place.x_other)
 
     def gate_copy(i):
         return remote(*((s_gate_out, s_cot.at[z, x]), (gate_out, cot.at[z]))[i], g_s.at[i], g_r.at[i], place.partner)
+
+    def up_store(i):
+        here, there = ((s_up_out, s_cot.at[z, x]), (up_out, cot.at[z]))[i]
+        return pltpu.make_async_copy(here, there, store_sem.at[10 + i])
 
     l_all = Gather(place, cot, s_cot, l_s, l_r, ls_s, ls_r, lx_s, lx_r)
 
@@ -681,52 +701,32 @@
     def _():
         kx_out[...] = k_sum.result(()).astype(BF16)
         kx_copy().start()
-        ks_sum.step(4)
-        s_gate_out[...], s_cot[z, x] = cotangents(ks_sum.result(()), s_pre)
+        s_gate_out[...], s_up_out[...] = cotangents(ks_sum.result(()), s_pre)
         for way in (0, 1):
             gate_next(way, 0).start()
         gate_copy(0).start()
-        l_all.begin_split()
+        l_all.begin_split(s_up_out)
+        up_store(0).start()
         kx_copy().wait_recv()
-        gate_out[...], cot[z] = cotangents(kx_out[...].astype(F32) + kx_into[...].astype(F32), pre)
+        gate_out[...], up_out[...] = cotangents(kx_out[...].astype(F32) + kx_into[...].astype(F32), pre)
         for way in (0, 1):
             gate_next(way, 1).start()
-        l_all.begin_whole()
+        l_all.begin_whole(up_out)
+        up_store(1).start()
         gate_copy(1).start()
-
-    j_all.step(1)
 
     @pl.when(teacher)
     def _():
         gate_copy(0).wait_recv()
         l_all.x_copy(0, 0).start()
 
-    tokens.drain()
     for apart in range(1, 8):
-        hand(apart).wait_send()
+        err_copy(apart).wait_send()
         for b in halves:
             d_copy(b, apart).wait_send()
-    b_sum.drain()
-    s_sum.drain()
-    for g in (0, 1):
-        bx_copy(g).wait_send()
-    loss.over_z()
+    d_partner().wait_send()
+    j_all.step(3)
     l_all.step(1)
-    j_all.step(2)
-    c_all.drain()
-    e_sum.drain()
-    l_all.step(2)
-    j_all.step(3)
-    loss.over_role()
-    d_partner().wait_send()
-    for apart in range(1, 8):
-        err_copy(apart).wait_send()
-    ex_copy().wait_send()
-    norm.drain()
-    l_all.step(3)
-    stat[...] = stat[...] + loss.result()
-    stores.append(pltpu.make_async_copy(stat, stat_out, store_sem.at[4]))
-    stores[-1].start()
     j_all.last()
 
     def lin_columns(b):
@@ -746,6 +746,14 @@
         stores.append(pltpu.make_async_copy(lin_err.at[:, b], lin_columns(b), store_sem.at[5 + b]))
         stores[-1].start()
 
+    c_all.drain()
+    e_sum.drain()
+    l_all.step(2)
+    ex_copy().wait_send()
+    norm.drain()
+    j_all.drain()
+    l_all.step(3)
+
     @pl.when(teacher)
     def _():
         gate_copy(1).wait_recv()
@@ -753,12 +761,7 @@
     l_all.last_split()
     l_all.last_whole()
     l_all.wait_pair()
-    for i, (here, there) in enumerate(parts_of(cot, s_cot, cot_out)):
-        stores.append(pltpu.make_async_copy(here, there, store_sem.at[10 + i]))
-        stores[-1].start()
-
-    loss.drain()
-    j_all.drain()
+
     for b in halves:
         lin_share(b).wait_send()
 
@@ -775,6 +778,7 @@
         err_store().wait()
         kx_copy().wait_send()
         for i in (0, 1):
+            up_store(i).wait()
             gate_copy(i).wait_send()
             for way in (0, 1):
                 gate_next(way, i).wait_send()
@@ -815,16 +819,17 @@
         exchange_kernel,
         out_shape=[
             array(2, Z, ROWS, QUARTER),
-            array(Z, ROWS, UNITS),
+            array(Z, ROWS, WHOLE),
+            array(Z, 2, ROWS, SPLIT),
             array(Z, ROWS, UNITS),
             array(2, Z, ROWS, QUARTER),
             array(Z, ROWS, LIN),
             array(8, 128, dtype=F32),
         ],
         in_specs=[anywhere] * 4,
-        out_specs=[anywhere] * 6,
+        out_specs=[anywhere] * 7,
         scratch_shapes=[
-            vmem(2, Z, ROWS, QUARTER), vmem(WIDTH, 2 * UNITS), vmem(UNITS, WIDTH), vmem(2, WIDTH, QUARTER),
+            vmem(2, Z, ROWS, QUARTER), vmem(WIDTH, 2 * UNITS), vmem(UNITS, WIDTH), vmem(2, WIDTH, QUARTER), vmem(WIDTH, UNITS),
             vmem(2, Z, ROWS, WHOLE, dtype=F32), vmem(2, 4, 2, ROWS, WHOLE), vmem(2, 4, 2, ROWS, WHOLE),
             vmem(2, ROWS, WHOLE), vmem(2, ROWS, WHOLE), vmem(2, ROWS, WHOLE, dtype=F32), vmem(Z, ROWS, WHOLE),
             vmem(2, 2, Z, ROWS, SPLIT, dtype=F32), vmem(2, 4, 2, ROWS, SPLIT), vmem(2, 4, 2, ROWS, SPLIT),
@@ -834,10 +839,10 @@
             vmem(2, Z, ROWS, QUARTER, dtype=F32), vmem(2, 4, 2, ROWS, QUARTER), vmem(2, 4, 2, ROWS, QUARTER),
             vmem(ROWS, QUARTER), vmem(ROWS, QUARTER), vmem(Z, 2, ROWS, QUARTER),
             vmem(2, 4, ROWS, WHOLE), vmem(2, 4, ROWS, WHOLE), vmem(ROWS, WHOLE), vmem(ROWS, WHOLE),
-            vmem(ROWS, WHOLE), vmem(Z, ROWS, WHOLE),
+            vmem(ROWS, WHOLE), vmem(ROWS, WHOLE),
             vmem(2, 4, ROWS, SPLIT), vmem(2, 4, ROWS, SPLIT), vmem(Z, ROWS, SPLIT), vmem(Z, ROWS, SPLIT),
-            vmem(ROWS, SPLIT), vmem(Z, 2, ROWS, SPLIT),
-            *total_tiles(), *total_tiles(), vmem(8, 128, dtype=F32),
+            vmem(ROWS, SPLIT), vmem(ROWS, SPLIT),
+            *total_tiles(), vmem(8, 128, dtype=F32),
             sems(6), sems(13),
             sems(7), sems(7), sems(7), sems(7), sems(2, 4, 2), sems(2, 4, 2), sems(3), sems(3),
             sems(2, 4, 2), sems(2, 4, 2), sems(8), sems(8),
@@ -847,11 +852,10 @@
             sems(2, 4, 2), sems(2, 4, 2), sems(1), sems(1),
             sems(2, 4), sems(2, 4), sems(2, 4), sems(2, 4), sems(8), sems(8), sems(2), sems(2), sems(2, 2),
             sems(7), sems(7), sems(7), sems(7), sems(2), sems(2),
-            sems(7), sems(7), sems(7), sems(7), sems(2), sems(2),
             sems(8), sems(8),
         ],
         compiler_params=pltpu.CompilerParams(
-            collective_id=0, has_side_effects=True, vmem_limit_bytes=34 * 1024 * 1024
+            collective_id=0, has_side_effects=True, vmem_limit_bytes=36 * 1024 * 1024
         ),
         name="exchange",
     )(tokens, w, down, linear)
@@ -864,7 +868,9 @@
 BLOCK = 256
 
 
-def gradients_kernel(tok, cot, hid, err, lin_err, stat, unit_out, down_out, linear_out, losses, turned, unit, down, linear, sem):
+def gradients_kernel(
+    tok, cot, s_cot, hid, err, lin_err, stat, unit_out, down_out, linear_out, losses, turned, unit, down, linear, sem
+):
     factor = (16.0 * MODEL) / stat[0:1, 0:1]
     share = stat[...] / stat[0:1, 0:1]
     losses[0] = share[1, 0]
@@ -879,7 +885,12 @@
 
     for i in range(UNITS // BLOCK):
         part = slice(i * BLOCK, (i + 1) * BLOCK)
-        unit[:, part] = jnp.dot(turned[...], cot[:, part], preferred_element_type=F32).astype(BF16)
+        split, column = divmod(i * BLOCK - WHOLE, SPLIT)
+        if split < 0:
+            columns = cot[:, part]
+        else:
+            columns = s_cot[:, split, :, column : column + BLOCK].reshape(Z * ROWS, BLOCK)
+        unit[:, part] = jnp.dot(turned[...], columns, preferred_element_type=F32).astype(BF16)
         send(unit.at[:, part], unit_out.at[:, part])
         for b in (0, 1):
             down[part, b * QUARTER : (b + 1) * QUARTER] = (factor * contract_rows(hid[:, part], err[b])).astype(BF16)
@@ -892,12 +903,12 @@
         copy.wait()
 
 
-def gradients(tok, cot, hid, err, lin_err, stat):
+def gradients(tok, cot, s_cot, hid, err, lin_err, stat):
     shapes = [(WIDTH, UNITS), (UNITS, WIDTH), (WIDTH, LIN)]
     return pl.pallas_call(
         gradients_kernel,
         out_shape=[jax.ShapeDtypeStruct(shape, BF16) for shape in shapes] + [jax.ShapeDtypeStruct((2,), F32)],
-        in_specs=[pl.BlockSpec(memory_space=pltpu.VMEM)] * 6,
+        in_specs=[pl.BlockSpec(memory_space=pltpu.VMEM)] * 7,
         out_specs=[pl.BlockSpec(memory_space=pl.ANY)] * 3 + [pl.BlockSpec(memory_space=pltpu.SMEM)],
         scratch_shapes=[
             pltpu.VMEM((WIDTH, Z * ROWS), BF16),
@@ -906,16 +917,17 @@
         ],
         compiler_params=pltpu.CompilerParams(vmem_limit_bytes=24 * 1024 * 1024),
         name="gradients",
-    )(tok, cot, hid, err, lin_err, stat)
+    )(tok, cot, s_cot, hid, err, lin_err, stat)
 
 
 def body(tokens, gate_up, down, linear):
     w = gate_up.reshape(WIDTH, 2 * UNITS)
-    tok, cot, hid, err, lin_err, stat = exchange(tokens, w, down[0], linear)
+    tok, cot, s_cot, hid, err, lin_err, stat = exchange(tokens, w, down[0], linear)
     rows = Z * ROWS
     unit_grad, down_grad, linear_grad, losses = gradients(
         tok.reshape(2, rows, QUARTER),
-        cot.reshape(rows, UNITS),
+        cot.reshape(rows, WHOLE),
+        s_cot,
         hid.reshape(rows, UNITS),
         err.reshape(2, rows, QUARTER),
         lin_err.reshape(rows, LIN),

time: 126 us -> 122 us (0.968)
  Pallas kernels: 123 us -> 119 us
    pallas_call x1, Pallas kernels: 119 us -> 115 us  [exchange(): pl.pallas_call(exchange_kernel, out_shape=[array(2, Z, ROWS, QUARTER), ar...]
where the time goes in v5:
time: 122 us
  Pallas kernels  119 us (98%)
  local copies, waits for them, and re-layouts  2.84 us (2%)
    pallas_call x1, Pallas kernels, exchange(): pl.pallas_call(exchange_kernel, out_shape=[array(2, Z, ROWS, QUARTER), ar...  115 us
    pallas_call x1, Pallas kernels, gradients(): pl.pallas_call(gradients_kernel, out_shape=[jax.ShapeDtypeStruct(shape, B...  4.11 us
    unnamed x7, local copies, waits for them, and re-layouts  2.84 us

profile of v5, /device:TPU:1, one launch (start us, length us, event | category | flops | bytes accessed | tf_op | source)
XLA Modules:
  0.0 122.3 jit_solution(13316163914493421467)
XLA Ops:
  0.6 0.0 copy-start
  0.6 0.0 copy-start.1
  0.7 0.0 copy-start.2
  0.7 2.8 %copy.8 = bf16[64,8,2,1792]{3,1,2,0:T(8,128)(2,1)S(1)} copy(bf16[64,8,2,1792]{3,2,1,0:T(2,128)(2,1)} %bitcast.17) | data formatting | bytes 7340032
  3.4 0.0 copy-done
  3.5 0.1 copy-done.1
  3.5 0.0 copy-done.2
  3.5 114.7 %exchange.1 = (bf16[2,8,48,256]{3,2,1,0:T(8,128)(2,1)S(1)}, bf16[8,48,768]{2,1,0:T(8,128)(2,1)S(1)}, bf16[8,2,48,512]{3,2,1,0:T(8,128)(2,1)S(1)}, bf16[8,48,1792...) custom-call(bf16[48,512]{1,0:T(8,128)(2,1)S(1)} %copy-done.2, ...), custom_call_target="tpu_custom_call" | custom-call | tf_op jit(solution)/shard_map/exchange/pallas_call | solution.py:818
  118.2 4.1 %gradients.1 = (bf16[512,1792]{1,0:T(8,128)(2,1)}, bf16[1792,512]{1,0:T(8,128)(2,1)}, bf16[512,1024]{1,0:T(8,128)(2,1)}, f32[2]{0:T(128)}) custom-call(bf16[2,384,256]{2,1,0:T(8,128)(2,1)S(1)} %bitcast.15, bf16[384,768]{1,0:T(8,128)(2,1)S(1)} %bitcast.14, bf16[8,2,48,512]{3,2,1,0:T(8,128)(2,1)S(1)} %get-tuple-element.17.s_cot, ...), custom_call_target="tpu_custom_call" | custom-call | tf_op jit(solution)/shard_map/gradients/pallas_call | solution.py:908
Async XLA Ops:
  0.6 2.8 %copy-start = (bf16[1,1792,512]{2,1,0:T(8,128)(2,1)S(1)}, bf16[1,1792,512]{2,1,0:T(8,128)(2,1)}, u32[]{:S(2)}) copy-start(bf16[1,1792,512]{2,1,0:T(8,128)(2,1)} %param.6) | copy-start | bytes 5505028
  0.6 2.9 %copy-start.1 = (bf16[512,1024]{1,0:T(8,128)(2,1)S(1)}, bf16[512,1024]{1,0:T(8,128)(2,1)}, u32[]{:S(2)}) copy-start(bf16[512,1024]{1,0:T(8,128)(2,1)} %lin_in.1) | copy-start | bytes 3145732
  0.7 2.9 %copy-start.2 = (bf16[48,512]{1,0:T(8,128)(2,1)S(1)}, bf16[48,512]{1,0:T(8,128)(2,1)}, u32[]{:S(2)}) copy-start(bf16[48,512]{1,0:T(8,128)(2,1)} %tok_in.1) | copy-start | bytes 147460

commit v6 on v5

--- a/solution.py
+++ b/solution.py
@@ -325,8 +325,8 @@
 
 def exchange_kernel(
     tok_in, w_in, down_in, lin_in,
-    tok_out, cot, s_cot, hid_out, err_out, lin_out, stat_out,
-    tok, w, down, lin, down_turned,
+    tok_out, cot, s_cot, down_out, linear_out, stat_out,
+    tok, w, down, lin, down_turned, hid_out, err_out, lin_out, down_grad, linear_grad,
     part, b_out, b_into, bx_out, bx_into, pre, hid,
     s_part, s_out, s_into, sx_out, sx_into, s_pre, s_hid,
     d_part, d_out, d_into, err, target_out, target,
@@ -622,10 +622,6 @@
         ks_sum.exchange((3, 5))
         s_part[1, 0] = cot_dot(pl.multiple_of(WHOLE + x_of[1] * SPLIT, 128), SPLIT)
         ks_sum.exchange((2, 6, 1, 7, 0))
-        err_share().start()
-        err_store().start()
-        for copy in hid_shares() + hid_stores():
-            copy.start()
 
     ex_copy().wait_recv()
 
@@ -666,6 +662,10 @@
         ks_sum.step(3)
         k_sum.step(4)
         ks_sum.step(4)
+        err_share().start()
+        err_store().start()
+        for copy in hid_shares() + hid_stores():
+            copy.start()
 
     norm.over_role()
     j_all.step(2)
@@ -741,18 +741,58 @@
         got = lin_out.at[:, :, pl.ds(start, QUARTER)]
         return remote(lin_err.at[:, b], got, share_s.at[3 + b], share_r.at[3 + b], place.partner)
 
+    lin_stores = [pltpu.make_async_copy(lin_err.at[:, b], lin_columns(b), store_sem.at[5 + b]) for b in halves]
     for b in halves:
         lin_share(b).start()
-        stores.append(pltpu.make_async_copy(lin_err.at[:, b], lin_columns(b), store_sem.at[5 + b]))
-        stores[-1].start()
-
+        lin_stores[b].start()
+
+    @pl.when(student)
+    def _():
+        err_store().wait()
+        for copy in hid_stores():
+            copy.wait()
+
+    @pl.when(teacher)
+    def _():
+        err_share().wait_recv()
+        for copy in hid_shares():
+            copy.wait_recv()
+
+    factor = (16.0 * MODEL) / stat[0:1, 0:1]
+
+    def rows_of(ref, c):
+        return ref[:, :, c * QUARTER : (c + 1) * QUARTER].reshape(Z * ROWS, QUARTER)
+
+    def down_piece(c):
+        for b in halves:
+            product = contract_rows(rows_of(hid_out, c), err_out[b].reshape(Z * ROWS, QUARTER))
+            down_grad[c * QUARTER : (c + 1) * QUARTER, b * QUARTER : (b + 1) * QUARTER] = (factor * product).astype(BF16)
+
+    def linear_piece(c):
+        for b in halves:
+            product = contract_rows(tok[b].reshape(Z * ROWS, QUARTER), rows_of(lin_out, c))
+            linear_grad[b * QUARTER : (b + 1) * QUARTER, c * QUARTER : (c + 1) * QUARTER] = (factor * product).astype(BF16)
+
+    for c in range(4):
+        down_piece(c)
     c_all.drain()
     e_sum.drain()
     l_all.step(2)
+    for c in range(4, UNITS // QUARTER):
+        down_piece(c)
+    stores.append(pltpu.make_async_copy(down_grad, down_out, store_sem.at[12]))
+    stores[-1].start()
     ex_copy().wait_send()
     norm.drain()
     j_all.drain()
     l_all.step(3)
+    for b in halves:
+        lin_arrival(b).wait_recv()
+        lin_stores[b].wait()
+    for c in range(LIN // QUARTER):
+        linear_piece(c)
+    stores.append(pltpu.make_async_copy(linear_grad, linear_out, store_sem.at[13]))
+    stores[-1].start()
 
     @pl.when(teacher)
     def _():
@@ -775,7 +815,6 @@
         ks_sum.drain()
         l_all.drain()
         err_share().wait_send()
-        err_store().wait()
         kx_copy().wait_send()
         for i in (0, 1):
             up_store(i).wait()
@@ -784,19 +823,12 @@
                 gate_next(way, i).wait_send()
         for copy in hid_shares():
             copy.wait_send()
-        for copy in hid_stores():
-            copy.wait()
 
     @pl.when(teacher)
     def _():
         l_all.drain(2)
         err_partner().wait_send()
-        err_share().wait_recv()
-        for copy in hid_shares():
-            copy.wait_recv()
-
-    for b in halves:
-        lin_arrival(b).wait_recv()
+
     for store in stores:
         store.wait()
 
@@ -821,15 +853,15 @@
             array(2, Z, ROWS, QUARTER),
             array(Z, ROWS, WHOLE),
             array(Z, 2, ROWS, SPLIT),
-            array(Z, ROWS, UNITS),
-            array(2, Z, ROWS, QUARTER),
-            array(Z, ROWS, LIN),
+            array(UNITS, WIDTH),
+            array(WIDTH, LIN),
             array(8, 128, dtype=F32),
         ],
         in_specs=[anywhere] * 4,
-        out_specs=[anywhere] * 7,
+        out_specs=[anywhere] * 6,
         scratch_shapes=[
             vmem(2, Z, ROWS, QUARTER), vmem(WIDTH, 2 * UNITS), vmem(UNITS, WIDTH), vmem(2, WIDTH, QUARTER), vmem(WIDTH, UNITS),
+            vmem(Z, ROWS, UNITS), vmem(2, Z, ROWS, QUARTER), vmem(Z, ROWS, LIN), vmem(UNITS, WIDTH), vmem(WIDTH, LIN),
             vmem(2, Z, ROWS, WHOLE, dtype=F32), vmem(2, 4, 2, ROWS, WHOLE), vmem(2, 4, 2, ROWS, WHOLE),
             vmem(2, ROWS, WHOLE), vmem(2, ROWS, WHOLE), vmem(2, ROWS, WHOLE, dtype=F32), vmem(Z, ROWS, WHOLE),
             vmem(2, 2, Z, ROWS, SPLIT, dtype=F32), vmem(2, 4, 2, ROWS, SPLIT), vmem(2, 4, 2, ROWS, SPLIT),
@@ -843,7 +875,7 @@
             vmem(2, 4, ROWS, SPLIT), vmem(2, 4, ROWS, SPLIT), vmem(Z, ROWS, SPLIT), vmem(Z, ROWS, SPLIT),
             vmem(ROWS, SPLIT), vmem(ROWS, SPLIT),
             *total_tiles(), vmem(8, 128, dtype=F32),
-            sems(6), sems(13),
+            sems(6), sems(14),
             sems(7), sems(7), sems(7), sems(7), sems(2, 4, 2), sems(2, 4, 2), sems(3), sems(3),
             sems(2, 4, 2), sems(2, 4, 2), sems(8), sems(8),
             sems(2, 4), sems(2, 4), sems(2, 4), sems(2, 4), sems(8), sems(8),
@@ -855,7 +887,7 @@
             sems(8), sems(8),
         ],
         compiler_params=pltpu.CompilerParams(
-            collective_id=0, has_side_effects=True, vmem_limit_bytes=36 * 1024 * 1024
+            collective_id=0, has_side_effects=True, vmem_limit_bytes=42 * 1024 * 1024
         ),
         name="exchange",
     )(tokens, w, down, linear)
@@ -869,20 +901,21 @@
 
 
 def gradients_kernel(
-    tok, cot, s_cot, hid, err, lin_err, stat, unit_out, down_out, linear_out, losses, turned, unit, down, linear, sem
+    tok, cot, s_cot, stat, down, linear, unit_out, down_out, linear_out, losses, turned, unit, sem
 ):
-    factor = (16.0 * MODEL) / stat[0:1, 0:1]
+    copies = []
+
+    def send(here, there):
+        copies.append(pltpu.make_async_copy(here, there, sem.at[len(copies)]))
+        copies[-1].start()
+
+    send(down, down_out)
+    send(linear, linear_out)
     share = stat[...] / stat[0:1, 0:1]
     losses[0] = share[1, 0]
     losses[1] = share[2, 0]
     for b in (0, 1):
         turned[b * QUARTER : (b + 1) * QUARTER] = tok[b].T
-    copies = []
-
-    def send(here, there):
-        copies.append(pltpu.make_async_copy(here, there, sem.at[len(copies)]))
-        copies[-1].start()
-
     for i in range(UNITS // BLOCK):
         part = slice(i * BLOCK, (i + 1) * BLOCK)
         split, column = divmod(i * BLOCK - WHOLE, SPLIT)
@@ -892,46 +925,35 @@
             columns = s_cot[:, split, :, column : column + BLOCK].reshape(Z * ROWS, BLOCK)
         unit[:, part] = jnp.dot(turned[...], columns, preferred_element_type=F32).astype(BF16)
         send(unit.at[:, part], unit_out.at[:, part])
-        for b in (0, 1):
-            down[part, b * QUARTER : (b + 1) * QUARTER] = (factor * contract_rows(hid[:, part], err[b])).astype(BF16)
-        send(down.at[part], down_out.at[part])
-        if i < LIN // BLOCK:
-            product = jnp.dot(turned[...], lin_err[:, part], preferred_element_type=F32)
-            linear[:, part] = (factor * product).astype(BF16)
-            send(linear.at[:, part], linear_out.at[:, part])
     for copy in copies:
         copy.wait()
 
 
-def gradients(tok, cot, s_cot, hid, err, lin_err, stat):
+def gradients(tok, cot, s_cot, stat, down, linear):
     shapes = [(WIDTH, UNITS), (UNITS, WIDTH), (WIDTH, LIN)]
+    whole = pl.BlockSpec(memory_space=pltpu.VMEM)
+    anywhere = pl.BlockSpec(memory_space=pl.ANY)
     return pl.pallas_call(
         gradients_kernel,
         out_shape=[jax.ShapeDtypeStruct(shape, BF16) for shape in shapes] + [jax.ShapeDtypeStruct((2,), F32)],
-        in_specs=[pl.BlockSpec(memory_space=pltpu.VMEM)] * 7,
-        out_specs=[pl.BlockSpec(memory_space=pl.ANY)] * 3 + [pl.BlockSpec(memory_space=pltpu.SMEM)],
+        in_specs=[whole] * 4 + [anywhere] * 2,
+        out_specs=[anywhere] * 3 + [pl.BlockSpec(memory_space=pltpu.SMEM)],
         scratch_shapes=[
             pltpu.VMEM((WIDTH, Z * ROWS), BF16),
-            *[pltpu.VMEM(shape, BF16) for shape in shapes],
-            pltpu.SemaphoreType.DMA((2 * (UNITS // BLOCK) + LIN // BLOCK,)),
+            pltpu.VMEM((WIDTH, UNITS), BF16),
+            pltpu.SemaphoreType.DMA((2 + UNITS // BLOCK,)),
         ],
         compiler_params=pltpu.CompilerParams(vmem_limit_bytes=24 * 1024 * 1024),
         name="gradients",
-    )(tok, cot, s_cot, hid, err, lin_err, stat)
+    )(tok, cot, s_cot, stat, down, linear)
 
 
 def body(tokens, gate_up, down, linear):
     w = gate_up.reshape(WIDTH, 2 * UNITS)
-    tok, cot, s_cot, hid, err, lin_err, stat = exchange(tokens, w, down[0], linear)
+    tok, cot, s_cot, down_own, linear_own, stat = exchange(tokens, w, down[0], linear)
     rows = Z * ROWS
     unit_grad, down_grad, linear_grad, losses = gradients(
-        tok.reshape(2, rows, QUARTER),
-        cot.reshape(rows, WHOLE),
-        s_cot,
-        hid.reshape(rows, UNITS),
-        err.reshape(2, rows, QUARTER),
-        lin_err.reshape(rows, LIN),
-        stat,
+        tok.reshape(2, rows, QUARTER), cot.reshape(rows, WHOLE), s_cot, stat, down_own, linear_own
     )
     return (unit_grad[None], down_grad, linear_grad, losses)
 

time: 122 us -> 121 us (level)
  Pallas kernels: 119 us -> 117 us
    pallas_call x1, Pallas kernels: 4.11 us -> 2.89 us  [gradients(): pl.pallas_call(gradients_kernel, out_shape=[jax.ShapeDtypeStruct(shape, B...]
where the time goes in v6:
time: 121 us
  Pallas kernels  117 us (97%)
  local copies, waits for them, and re-layouts  2.84 us (2%)
    pallas_call x1, Pallas kernels, exchange(): pl.pallas_call(exchange_kernel, out_shape=[array(2, Z, ROWS, QUARTER), ar...  114 us
    pallas_call x1, Pallas kernels, gradients(): pl.pallas_call(gradients_kernel, out_shape=[jax.ShapeDtypeStruct(shape, B...  2.89 us
    unnamed x7, local copies, waits for them, and re-layouts  2.84 us

profile of v6, /device:TPU:1, one launch (start us, length us, event | category | flops | bytes accessed | tf_op | source)
XLA Modules:
  0.0 120.8 jit_solution(8214359159128362899)
XLA Ops:
  0.6 0.0 copy-start
  0.6 0.0 copy-start.1
  0.7 0.0 copy-start.2
  0.7 2.8 %copy.8 = bf16[64,8,2,1792]{3,1,2,0:T(8,128)(2,1)S(1)} copy(bf16[64,8,2,1792]{3,2,1,0:T(2,128)(2,1)} %bitcast.11) | data formatting | bytes 7340032
  3.4 0.0 copy-done
  3.5 0.1 copy-done.1
  3.5 0.0 copy-done.2
  3.5 114.4 %exchange.1 = (bf16[2,8,48,256]{3,2,1,0:T(8,128)(2,1)S(1)}, bf16[8,48,768]{2,1,0:T(8,128)(2,1)S(1)}, bf16[8,2,48,512]{3,2,1,0:T(8,128)(2,1)S(1)}, bf16[1792,512]...) custom-call(bf16[48,512]{1,0:T(8,128)(2,1)S(1)} %copy-done.2, bf16[512,3584]{1,0:T(8,128)(2,1)S(1)} %bitcast.7, ...), custom_call_target="tpu_custom_call" | custom-call | tf_op jit(solution)/shard_map/exchange/pallas_call | solution.py:850
  118.0 2.9 %gradients.1 = (bf16[512,1792]{1,0:T(8,128)(2,1)}, bf16[1792,512]{1,0:T(8,128)(2,1)}, bf16[512,1024]{1,0:T(8,128)(2,1)}, f32[2]{0:T(128)}) custom-call(bf16[2,384,256]{2,1,0:T(8,128)(2,1)S(1)} %bitcast.10, bf16[384,768]{1,0:T(8,128)(2,1)S(1)} %bitcast.9, bf16[8,2,48,512]{3,2,1,0:T(8,128)(2,1)S(1)} %get-tuple-element.16.s_cot, ...), custom_call_target="tpu_custom_call" | custom-call | tf_op jit(solution)/shard_map/gradients/pallas_call | solution.py:936
Async XLA Ops:
  0.6 2.8 %copy-start = (bf16[1,1792,512]{2,1,0:T(8,128)(2,1)S(1)}, bf16[1,1792,512]{2,1,0:T(8,128)(2,1)}, u32[]{:S(2)}) copy-start(bf16[1,1792,512]{2,1,0:T(8,128)(2,1)} %param.6) | copy-start | bytes 5505028
  0.6 2.9 %copy-start.1 = (bf16[512,1024]{1,0:T(8,128)(2,1)S(1)}, bf16[512,1024]{1,0:T(8,128)(2,1)}, u32[]{:S(2)}) copy-start(bf16[512,1024]{1,0:T(8,128)(2,1)} %lin_in.1) | copy-start | bytes 3145732
  0.7 2.9 %copy-start.2 = (bf16[48,512]{1,0:T(8,128)(2,1)S(1)}, bf16[48,512]{1,0:T(8,128)(2,1)}, u32[]{:S(2)}) copy-start(bf16[48,512]{1,0:T(8,128)(2,1)} %tok_in.1) | copy-start | bytes 147460

commit v7 on v6

--- a/solution.py
+++ b/solution.py
@@ -326,7 +326,7 @@
 def exchange_kernel(
     tok_in, w_in, down_in, lin_in,
     tok_out, cot, s_cot, down_out, linear_out, stat_out,
-    tok, w, down, lin, down_turned, hid_out, err_out, lin_out, down_grad, linear_grad,
+    tok, w, down, lin, down_turned, tok_turned, hid_out, err_out, lin_out, down_grad, linear_grad,
     part, b_out, b_into, bx_out, bx_into, pre, hid,
     s_part, s_out, s_into, sx_out, sx_into, s_pre, s_hid,
     d_part, d_out, d_into, err, target_out, target,
@@ -406,8 +406,6 @@
     loads[2].wait()
     for apart in (1, 7, 2, 6, 3, 5, 4):
         hand(apart, True).wait_recv()
-    stores = [pltpu.make_async_copy(tok, tok_out, store_sem.at[0])]
-    stores[0].start()
 
     def all_tokens():
         return jnp.concatenate([tok[b].reshape(Z * ROWS, QUARTER) for b in halves], axis=1)
@@ -447,6 +445,10 @@
     s_sum.exchange((1, 7, 0))
     for c in range(UNITS // QUARTER):
         down_turned[:, c * QUARTER : (c + 1) * QUARTER] = down[c * QUARTER : (c + 1) * QUARTER].T
+    for b in halves:
+        tok_turned[b * QUARTER : (b + 1) * QUARTER] = tok[b].reshape(Z * ROWS, QUARTER).T
+    stores = [pltpu.make_async_copy(tok_turned, tok_out, store_sem.at[0])]
+    stores[0].start()
     s_sum.step(3)
     b_sum.step(4)
     s_sum.step(4)
@@ -749,8 +751,13 @@
     @pl.when(student)
     def _():
         err_store().wait()
+        err_share().wait_send()
         for copy in hid_stores():
             copy.wait()
+        for copy in hid_shares():
+            copy.wait_send()
+        k_sum.drain()
+        ks_sum.drain()
 
     @pl.when(teacher)
     def _():
@@ -770,7 +777,9 @@
 
     def linear_piece(c):
         for b in halves:
-            product = contract_rows(tok[b].reshape(Z * ROWS, QUARTER), rows_of(lin_out, c))
+            product = jnp.dot(
+                tok_turned[b * QUARTER : (b + 1) * QUARTER], rows_of(lin_out, c), preferred_element_type=F32
+            )
             linear_grad[b * QUARTER : (b + 1) * QUARTER, c * QUARTER : (c + 1) * QUARTER] = (factor * product).astype(BF16)
 
     for c in range(4):
@@ -811,18 +820,13 @@
 
     @pl.when(student)
     def _():
-        k_sum.drain()
-        ks_sum.drain()
         l_all.drain()
-        err_share().wait_send()
         kx_copy().wait_send()
         for i in (0, 1):
             up_store(i).wait()
             gate_copy(i).wait_send()
             for way in (0, 1):
                 gate_next(way, i).wait_send()
-        for copy in hid_shares():
-            copy.wait_send()
 
     @pl.when(teacher)
     def _():
@@ -850,7 +854,7 @@
     return pl.pallas_call(
         exchange_kernel,
         out_shape=[
-            array(2, Z, ROWS, QUARTER),
+            array(WIDTH, Z * ROWS),
             array(Z, ROWS, WHOLE),
             array(Z, 2, ROWS, SPLIT),
             array(UNITS, WIDTH),
@@ -860,7 +864,7 @@
         in_specs=[anywhere] * 4,
         out_specs=[anywhere] * 6,
         scratch_shapes=[
-            vmem(2, Z, ROWS, QUARTER), vmem(WIDTH, 2 * UNITS), vmem(UNITS, WIDTH), vmem(2, WIDTH, QUARTER), vmem(WIDTH, UNITS),
+            vmem(2, Z, ROWS, QUARTER), vmem(WIDTH, 2 * UNITS), vmem(UNITS, WIDTH), vmem(2, WIDTH, QUARTER), vmem(WIDTH, UNITS), vmem(WIDTH, Z * ROWS),
             vmem(Z, ROWS, UNITS), vmem(2, Z, ROWS, QUARTER), vmem(Z, ROWS, LIN), vmem(UNITS, WIDTH), vmem(WIDTH, LIN),
             vmem(2, Z, ROWS, WHOLE, dtype=F32), vmem(2, 4, 2, ROWS, WHOLE), vmem(2, 4, 2, ROWS, WHOLE),
             vmem(2, ROWS, WHOLE), vmem(2, ROWS, WHOLE), vmem(2, ROWS, WHOLE, dtype=F32), vmem(Z, ROWS, WHOLE),
@@ -901,7 +905,7 @@
 
 
 def gradients_kernel(
-    tok, cot, s_cot, stat, down, linear, unit_out, down_out, linear_out, losses, turned, unit, sem
+    turned, cot, s_cot, stat, down, linear, unit_out, down_out, linear_out, losses, unit, sem
 ):
     copies = []
 
@@ -914,8 +918,6 @@
     share = stat[...] / stat[0:1, 0:1]
     losses[0] = share[1, 0]
     losses[1] = share[2, 0]
-    for b in (0, 1):
-        turned[b * QUARTER : (b + 1) * QUARTER] = tok[b].T
     for i in range(UNITS // BLOCK):
         part = slice(i * BLOCK, (i + 1) * BLOCK)
         split, column = divmod(i * BLOCK - WHOLE, SPLIT)
@@ -929,7 +931,7 @@
         copy.wait()
 
 
-def gradients(tok, cot, s_cot, stat, down, linear):
+def gradients(turned, cot, s_cot, stat, down, linear):
     shapes = [(WIDTH, UNITS), (UNITS, WIDTH), (WIDTH, LIN)]
     whole = pl.BlockSpec(memory_space=pltpu.VMEM)
     anywhere = pl.BlockSpec(memory_space=pl.ANY)
@@ -939,13 +941,12 @@
         in_specs=[whole] * 4 + [anywhere] * 2,
         out_specs=[anywhere] * 3 + [pl.BlockSpec(memory_space=pltpu.SMEM)],
         scratch_shapes=[
-            pltpu.VMEM((WIDTH, Z * ROWS), BF16),
             pltpu.VMEM((WIDTH, UNITS), BF16),
             pltpu.SemaphoreType.DMA((2 + UNITS // BLOCK,)),
         ],
         compiler_params=pltpu.CompilerParams(vmem_limit_bytes=24 * 1024 * 1024),
         name="gradients",
-    )(tok, cot, s_cot, stat, down, linear)
+    )(turned, cot, s_cot, stat, down, linear)
 
 
 def body(tokens, gate_up, down, linear):
@@ -953,7 +954,7 @@
     tok, cot, s_cot, down_own, linear_own, stat = exchange(tokens, w, down[0], linear)
     rows = Z * ROWS
     unit_grad, down_grad, linear_grad, losses = gradients(
-        tok.reshape(2, rows, QUARTER), cot.reshape(rows, WHOLE), s_cot, stat, down_own, linear_own
+        tok, cot.reshape(rows, WHOLE), s_cot, stat, down_own, linear_own
     )
     return (unit_grad[None], down_grad, linear_grad, losses)
 

time: 121 us -> 121 us (level)
  no operation moved by 1% of the time
where the time goes in v7:
time: 121 us
  Pallas kernels  117 us (97%)
  local copies, waits for them, and re-layouts  2.84 us (2%)
    pallas_call x1, Pallas kernels, exchange(): pl.pallas_call(exchange_kernel, out_shape=[array(WIDTH, Z * ROWS), array(...  114 us
    pallas_call x1, Pallas kernels, gradients(): pl.pallas_call(gradients_kernel, out_shape=[jax.ShapeDtypeStruct(shape, B...  2.9 us
    unnamed x7, local copies, waits for them, and re-layouts  2.84 us

profile of v7, /device:TPU:1, one launch (start us, length us, event | category | flops | bytes accessed | tf_op | source)
XLA Modules:
  0.0 120.6 jit_solution(11141952444968370892)
XLA Ops:
  0.6 0.0 copy-start
  0.6 0.0 copy-start.1
  0.7 0.0 copy-start.2
  0.7 2.8 %copy.8 = bf16[64,8,2,1792]{3,1,2,0:T(8,128)(2,1)S(1)} copy(bf16[64,8,2,1792]{3,2,1,0:T(2,128)(2,1)} %bitcast.9) | data formatting | bytes 7340032
  3.4 0.0 copy-done
  3.5 0.1 copy-done.1
  3.5 0.0 copy-done.2
  3.5 114.1 %exchange.1 = (bf16[512,384]{1,0:T(8,128)(2,1)S(1)}, bf16[8,48,768]{2,1,0:T(8,128)(2,1)S(1)}, bf16[8,2,48,512]{3,2,1,0:T(8,128)(2,1)S(1)}, bf16[1792,512]{1,0:T(...) custom-call(bf16[48,512]{1,0:T(8,128)(2,1)S(1)} %copy-done.2, bf16[512,3584]{1,0:T(8,128)(2,1)S(1)} %bitcast.6, ...), custom_call_target="tpu_custom_call" | custom-call | tf_op jit(solution)/shard_map/exchange/pallas_call | solution.py:854
  117.7 2.9 %gradients.1 = (bf16[512,1792]{1,0:T(8,128)(2,1)}, bf16[1792,512]{1,0:T(8,128)(2,1)}, bf16[512,1024]{1,0:T(8,128)(2,1)}, f32[2]{0:T(128)}) custom-call(bf16[512,384]{1,0:T(8,128)(2,1)S(1)} %get-tuple-element.14.turned, bf16[384,768]{1,0:T(8,128)(2,1)S(1)} %bitcast.8, bf16[8,2,48,512]{3,2,1,0:T(8,128)(2,1)S(1)} %get-tuple-element.16.s_cot, ...), custom_call_target="tpu_custom_call" | custom-call | tf_op jit(solution)/shard_map/gradients/pallas_call | solution.py:938
Async XLA Ops:
  0.6 2.8 %copy-start = (bf16[1,1792,512]{2,1,0:T(8,128)(2,1)S(1)}, bf16[1,1792,512]{2,1,0:T(8,128)(2,1)}, u32[]{:S(2)}) copy-start(bf16[1,1792,512]{2,1,0:T(8,128)(2,1)} %param.6) | copy-start | bytes 5505028
  0.6 2.9 %copy-start.1 = (bf16[512,1024]{1,0:T(8,128)(2,1)S(1)}, bf16[512,1024]{1,0:T(8,128)(2,1)}, u32[]{:S(2)}) copy-start(bf16[512,1024]{1,0:T(8,128)(2,1)} %lin_in.1) | copy-start | bytes 3145732
  0.7 2.9 %copy-start.2 = (bf16[48,512]{1,0:T(8,128)(2,1)S(1)}, bf16[48,512]{1,0:T(8,128)(2,1)}, u32[]{:S(2)}) copy-start(bf16[48,512]{1,0:T(8,128)(2,1)} %tok_in.1) | copy-start | bytes 147460

commit v8 on v7

--- a/solution.py
+++ b/solution.py
@@ -782,19 +782,21 @@
             )
             linear_grad[b * QUARTER : (b + 1) * QUARTER, c * QUARTER : (c + 1) * QUARTER] = (factor * product).astype(BF16)
 
-    for c in range(4):
+    for c in range(2):
         down_piece(c)
     c_all.drain()
     e_sum.drain()
     l_all.step(2)
-    for c in range(4, UNITS // QUARTER):
+    for c in range(2, 5):
         down_piece(c)
-    stores.append(pltpu.make_async_copy(down_grad, down_out, store_sem.at[12]))
-    stores[-1].start()
     ex_copy().wait_send()
     norm.drain()
     j_all.drain()
     l_all.step(3)
+    for c in range(5, UNITS // QUARTER):
+        down_piece(c)
+    stores.append(pltpu.make_async_copy(down_grad, down_out, store_sem.at[12]))
+    stores[-1].start()
     for b in halves:
         lin_arrival(b).wait_recv()
         lin_stores[b].wait()

time: 121 us -> 121 us (level)
  no operation moved by 1% of the time
where the time goes in v8:
time: 121 us
  Pallas kernels  117 us (97%)
  local copies, waits for them, and re-layouts  2.84 us (2%)
    pallas_call x1, Pallas kernels, exchange(): pl.pallas_call(exchange_kernel, out_shape=[array(WIDTH, Z * ROWS), array(...  115 us
    pallas_call x1, Pallas kernels, gradients(): pl.pallas_call(gradients_kernel, out_shape=[jax.ShapeDtypeStruct(shape, B...  2.9 us
    unnamed x7, local copies, waits for them, and re-layouts  2.84 us

profile of v8, /device:TPU:1, one launch (start us, length us, event | category | flops | bytes accessed | tf_op | source)
XLA Modules:
  0.0 121.0 jit_solution(7080116546471436712)
XLA Ops:
  0.6 0.0 copy-start
  0.6 0.0 copy-start.1
  0.7 0.0 copy-start.2
  0.7 2.8 %copy.8 = bf16[64,8,2,1792]{3,1,2,0:T(8,128)(2,1)S(1)} copy(bf16[64,8,2,1792]{3,2,1,0:T(2,128)(2,1)} %bitcast.9) | data formatting | bytes 7340032
  3.4 0.0 copy-done
  3.5 0.1 copy-done.1
  3.5 0.0 copy-done.2
  3.5 114.6 %exchange.1 = (bf16[512,384]{1,0:T(8,128)(2,1)S(1)}, bf16[8,48,768]{2,1,0:T(8,128)(2,1)S(1)}, bf16[8,2,48,512]{3,2,1,0:T(8,128)(2,1)S(1)}, bf16[1792,512]{1,0:T(...) custom-call(bf16[48,512]{1,0:T(8,128)(2,1)S(1)} %copy-done.2, bf16[512,3584]{1,0:T(8,128)(2,1)S(1)} %bitcast.6, ...), custom_call_target="tpu_custom_call" | custom-call | tf_op jit(solution)/shard_map/exchange/pallas_call | solution.py:856
  118.1 2.9 %gradients.1 = (bf16[512,1792]{1,0:T(8,128)(2,1)}, bf16[1792,512]{1,0:T(8,128)(2,1)}, bf16[512,1024]{1,0:T(8,128)(2,1)}, f32[2]{0:T(128)}) custom-call(bf16[512,384]{1,0:T(8,128)(2,1)S(1)} %get-tuple-element.14.turned, bf16[384,768]{1,0:T(8,128)(2,1)S(1)} %bitcast.8, bf16[8,2,48,512]{3,2,1,0:T(8,128)(2,1)S(1)} %get-tuple-element.16.s_cot, ...), custom_call_target="tpu_custom_call" | custom-call | tf_op jit(solution)/shard_map/gradients/pallas_call | solution.py:940
Async XLA Ops:
  0.6 2.8 %copy-start = (bf16[1,1792,512]{2,1,0:T(8,128)(2,1)S(1)}, bf16[1,1792,512]{2,1,0:T(8,128)(2,1)}, u32[]{:S(2)}) copy-start(bf16[1,1792,512]{2,1,0:T(8,128)(2,1)} %param.6) | copy-start | bytes 5505028
  0.6 2.9 %copy-start.1 = (bf16[512,1024]{1,0:T(8,128)(2,1)S(1)}, bf16[512,1024]{1,0:T(8,128)(2,1)}, u32[]{:S(2)}) copy-start(bf16[512,1024]{1,0:T(8,128)(2,1)} %lin_in.1) | copy-start | bytes 3145732
  0.7 2.9 %copy-start.2 = (bf16[48,512]{1,0:T(8,128)(2,1)S(1)}, bf16[48,512]{1,0:T(8,128)(2,1)}, u32[]{:S(2)}) copy-start(bf16[48,512]{1,0:T(8,128)(2,1)} %tok_in.1) | copy-start | bytes 147460
